TPU v7x, 128 devices: a whole 4x4x4 slice. The times are simulated.
128 devices in a mesh: comp: 4 (over y_hi, core), tile: 32 (over x, z, y_lo).
Axes of the slice: x: 4, y: 4 (y_hi: 2, y_lo: 2; y = y_hi * 2 + y_lo), z: 4, core: 2. Of those that a mesh axis runs over, the one named last changes fastest.
Arguments:
- state: float32 [4, 32, 3, 64, 2048], P('comp', 'tile'), may hold values from -6 to 6
- metric: float32 [4, 32, 2048], P('comp', 'tile'), may hold values from 0.5 to 2
- column_op: float32 [4, 64, 64], P('comp'), may hold values from -0.009375 to 1.0125
- links: int32 [4, 32, 6, 2048], P('comp', 'tile'), may hold values from -1 to 2303, as said below
- rims: int32 [4, 32, 2, 128], P('comp', 'tile'), may hold values from 0 to 2047
- out_map: int32 [4, 32, 32, 2, 128], P('comp', 'tile'), may hold values from -1 to 2047, as said below
- out_weight: float32 [4, 32, 32, 128], P('comp', 'tile'), may hold values from 0.25 to 1
- back_map: int32 [4, 32, 32, 2, 128], P('comp', 'tile'), may hold values from -1 to 2047, as said below
- back_weight: float32 [4, 32, 32, 128], P('comp', 'tile'), may hold values from 0.25 to 1
Outputs:
- new_state: float32 [4, 32, 3, 64, 2048], P('comp', 'tile')
Inputs may be any that keep to these rules, and one draw needn't show every extreme that they name: -1 marks no link; others are positions in the extended block of 2304 entries. Atmosphere nodes have 3 links at element corners, 1 on element edges, none inside (rows 3 to 5 are -1); ocean cells have 6. `out_map`: source node and target cell are -1 together, exactly in the slots at or beyond a pair's count of rows; a pair carries at most 128 rows, and for each atmosphere group c some ocean tile receives 128 rows from every block of c; the ocean tiles' entries are all -1. `back_map`: source cell and target node are -1 together, exactly in the slots at or beyond a pair's count of rows; a pair carries at most 128 rows, and for each atmosphere group c some block of c receives 128 rows from every ocean tile; the ocean tiles' entries are all -1.
All inputs are finite; a program needn't handle non-finite values.
Results may differ from a plain program's by a relative error of at most 0.0003.
Values sent between devices are 32-bit elements; how exact they have to be, the bound alone decides.
No kernel may reach another device: no remote copies, remote signals or barrier semaphores. Data moves between devices by JAX's collectives and lax.ppermute only.
A program may use at most 256 MiB of HBM per device.

v0:
```python
import math

import jax
import jax.numpy as jnp
import numpy as np
from jax import lax
from jax.sharding import PartitionSpec as P

VISCOSITY = 0.05
ATM_STEP = 0.02
OCEAN_RATE = 0.08
COUPLING = 0.5


def extended_2(cells, sides, width, closed):
    for axis, dim in sides:
        count = lax.axis_size(axis)
        ends = count if closed else count - 1
        head = lax.slice_in_dim(cells, 0, width, axis=dim)
        tail = lax.slice_in_dim(cells, cells.shape[dim] - width, cells.shape[dim], axis=dim)
        cells = jnp.concatenate(
            [
                lax.ppermute(tail, axis, [(i, (i + 1) % count) for i in range(ends)]),
                cells,
                lax.ppermute(head, axis, [((i + 1) % count, i) for i in range(ends)]),
            ],
            axis=dim,
        )
    return cells


def gll_blocks():
    points = np.array([-1.0, -1.0 / math.sqrt(5.0), 1.0 / math.sqrt(5.0), 1.0])
    legendre = 0.5 * (5.0 * points * points * points - 3.0 * points)
    matrix = np.zeros((4, 4))
    for first_point in range(4):
        for second_point in range(4):
            if first_point != second_point:
                matrix[first_point, second_point] = legendre[first_point] / (
                    legendre[second_point] * (points[first_point] - points[second_point])
                )
    matrix[0, 0] = -3.0
    matrix[3, 3] = 3.0
    along_xi = np.kron(np.eye(4), matrix)
    along_eta = np.kron(matrix, np.eye(4))
    return (
        jnp.asarray(np.kron(np.eye(8), along_xi), dtype=jnp.float32),
        jnp.asarray(np.kron(np.eye(8), along_eta), dtype=jnp.float32),
    )


def apply_block(values, block):
    shape = values.shape
    grouped = values.reshape(shape[:-1] + (shape[-1] // 128, 128))
    result = jnp.einsum("...m,nm->...n", grouped, block, precision=lax.Precision.HIGHEST)
    return result.reshape(shape)


def atmos_tendency(current, metric):
    block_xi, block_eta = gll_blocks()
    grad_xi = apply_block(current, block_xi)
    grad_eta = apply_block(current, block_eta)
    second = apply_block(grad_xi, block_xi) + apply_block(grad_eta, block_eta)
    wind_u = current[0][None]
    wind_v = current[1][None]
    return -metric * (wind_u * grad_xi + wind_v * grad_eta) + VISCOSITY * metric * metric * second


def pack_rows(values, sources, weight):
    picked = jnp.take(values, jnp.maximum(sources, 0), axis=1)
    return jnp.where(sources >= 0, picked, 0.0) * weight


def land_rows(rows, cells, count):
    block = 512
    cells_col = cells[:, None]

    def land_block(which, total):
        start = which * block
        targets = start + jnp.arange(block, dtype=jnp.int32)[None, :]
        onehot = (cells_col == targets).astype(jnp.float32)
        landed = jnp.dot(
            rows, onehot, precision=lax.Precision.HIGHEST, preferred_element_type=jnp.float32
        )
        return lax.dynamic_update_slice_in_dim(total, landed, start, 1)

    empty = jnp.zeros((rows.shape[0], count), jnp.float32)
    return lax.fori_loop(0, count // block, land_block, empty)


def linked_rows(extended, links):
    total = jnp.zeros(extended.shape[:2] + (links.shape[1],), jnp.float32)
    for which in range(links.shape[0]):
        index = links[which]
        picked = jnp.take(extended, jnp.maximum(index, 0), axis=2)
        total = total + jnp.where(index >= 0, picked, 0.0)
    number = jnp.sum((links >= 0).astype(jnp.float32), axis=0)
    return (total, number)


def finish(updated, forcing, column):
    mixed = jnp.einsum("kl,fln->fkn", column, updated, precision=lax.Precision.HIGHEST)
    return mixed + COUPLING * column[:, 0][None, :, None] * forcing[:, None, :]


def per_device(state, metric, column_op, links, rims, out_map, out_weight, back_map, back_weight):
    current = state[0, 0]
    metric_one = metric[0, 0]
    column = column_op[0]
    link_rows = links[0, 0]
    rim_rows = rims[0, 0]
    out_table = out_map[0, 0]
    out_scale = out_weight[0, 0]
    back_table = back_map[0, 0]
    back_scale = back_weight[0, 0]
    fields, levels, nodes = current.shape
    rim = rim_rows.shape[1]
    comp_index = lax.axis_index("comp")
    tile_index = lax.axis_index("tile")
    ncomp = lax.axis_size("comp")
    ntile = lax.axis_size("tile")
    is_ocean = comp_index == ncomp - 1
    surface = current[:, 0, :]
    sent_rows = pack_rows(surface, out_table[:, 0, :], out_scale)
    sent_cells = out_table[:, 1, :].astype(jnp.float32)[None]
    got_rows, got_cells = (
        lax.all_to_all(sent_rows, "tile", split_axis=1, concat_axis=1, tiled=True),
        lax.all_to_all(sent_cells, "tile", split_axis=1, concat_axis=1, tiled=True),
    )
    partial_value = land_rows(
        got_rows.reshape(fields, -1), got_cells.reshape(-1).astype(jnp.int32), nodes
    )
    partial_value = jnp.where(is_ocean, 0.0, partial_value)
    sea_part = jnp.where(is_ocean, surface, 0.0)
    forcing_ocean, sea_all = lax.psum((partial_value, sea_part), "comp")
    back_rows = pack_rows(sea_all, back_table[:, 0, :], back_scale)
    back_cells = back_table[:, 1, :].astype(jnp.float32)[None]
    got_back, got_back_cells = (
        lax.all_to_all(back_rows, "tile", split_axis=1, concat_axis=1, tiled=True),
        lax.all_to_all(back_cells, "tile", split_axis=1, concat_axis=1, tiled=True),
    )
    forcing_atmos = land_rows(
        got_back.reshape(fields, -1), got_back_cells.reshape(-1).astype(jnp.int32), nodes
    )
    forcing = jnp.where(is_ocean, forcing_ocean, forcing_atmos)
    field = lax.cond(
        is_ocean,
        lambda packed: packed[0],
        lambda packed: atmos_tendency(packed[0], packed[1]),
        (current, metric_one),
    )
    node_ids = jnp.arange(nodes, dtype=jnp.int32)[:, None]
    rim_table = (node_ids == rim_rows.reshape(-1)[None, :]).astype(jnp.float32)
    outgoing = jnp.einsum("fln,nr->flr", field, rim_table, precision=lax.Precision.HIGHEST)
    widened = extended_2(outgoing, (("tile", 2),), rim, True)
    left_in = widened[:, :, :rim]
    right_in = widened[:, :, 3 * rim :]
    crossing = extended_2(jnp.concatenate([right_in, left_in], axis=2), (("comp", 2),), rim, False)
    cross_left = crossing[:, :, :rim]
    cross_right = crossing[:, :, 3 * rim :]
    atmos_left = jnp.where(tile_index == 0, cross_left, left_in)
    atmos_right = jnp.where(
        tile_index == ntile - 1, jnp.where(comp_index == ncomp - 2, 0.0, cross_right), right_in
    )
    ocean_left = jnp.where(tile_index == 0, 0.0, left_in)
    ocean_right = jnp.where(tile_index == ntile - 1, 0.0, right_in)
    left = jnp.where(is_ocean, ocean_left, atmos_left)
    right = jnp.where(is_ocean, ocean_right, atmos_right)
    extended = jnp.concatenate([left, field, right], axis=2)
    linked, number = linked_rows(extended, link_rows)
    updated = lax.cond(
        is_ocean,
        lambda packed: packed[0] + OCEAN_RATE * packed[3] * (packed[2] - packed[4] * packed[0]),
        lambda packed: packed[0] + ATM_STEP * (packed[1] + packed[2]) / (1.0 + packed[4]),
        (current, field, linked, metric_one, number),
    )
    result = finish(updated, forcing, column)
    return result[None, None]


def solution(mesh):
    return jax.shard_map(
        per_device,
        mesh=mesh,
        in_specs=(
            P("comp", "tile", None, None, None),
            P("comp", "tile", None),
            P("comp", None, None),
            P("comp", "tile", None, None),
            P("comp", "tile", None, None),
            P("comp", "tile", None, None, None),
            P("comp", "tile", None, None),
            P("comp", "tile", None, None, None),
            P("comp", "tile", None, None),
        ),
        out_specs=P("comp", "tile", None, None, None),
        check_vma=False,
    )
```

profile of v0, /device:TPU:17, one launch (start us, length us, event | category | flops | bytes accessed | tf_op | source)
XLA Modules:
  0.0 480.2 jit_solution(1022180752434214064)
XLA Ops:
  0.0 32.9 %copy.67 = f32[1,1,3,64,2048]{2,4,3,1,0:T(8,128)} copy(f32[1,1,3,64,2048]{4,3,2,1,0:T(8,128)} %param.23) | data formatting | bytes 3145728 | tf_op args[0]
  32.9 0.1 conditional.2
  32.9 0.1 copy.122
  33.0 0.0 copy-start.8
  33.0 0.0 copy-start.3
  33.0 0.5 copy-done.12
  33.6 1.1 fusion.42
  34.7 6.7 %collective-permute-start.2 = (f32[3,64,128]{2,1,0:T(8,128)S(1)}, f32[3,64,128]{2,1,0:T(8,128)S(1)}, u32[]{:S(2)}, u32[]{:S(2)}) collective-permute-start(f32[3,64,128]{2,1,0:T(8,128)S(1)} %get-tuple-element.317), channel_id=1, source_target_pairs={{1,0},{2,1},{3,2},{4,3},{5,4},{6,5},{7,6},{8,7},{9,8},{10,9},{11,1... | collective-permute-start | bytes 294920 | tf_op jit(solution)/shard_map/ppermute | solution.py:25
  41.5 0.0 collective-permute-start
  41.5 0.6 slice_convert_fusion.1
  42.1 7.3 %all-to-all-start = ((f32[1,32,128]{2,0,1:T(1,128)}), f32[1,32,128]{2,0,1:T(1,128)S(1)}, u32[]{:S(2)}, u32[]{:S(2)}) async-start(f32[1,32,128]{2,0,1:T(1,128)} %bitcast.26), calls=%async_computation | async-start | bytes 32768 | tf_op jit(solution)/shard_map/all_to_all | solution.py:128
  49.4 0.1 slice_maximum_fusion.5
  49.6 0.2 compare_reduce_fusion.5
  49.8 0.1 fusion.48
  49.9 2.3 slice_bitcast_fusion.2
  52.2 1.3 broadcast_select_fusion
  53.5 0.0 copy-start.10
  53.5 0.0 copy-start.6
  53.6 0.6 slice_convert_fusion
  54.2 15.3 %gather_fusion.6 = f32[4096,3]{1,0:T(8,128)} fusion(f32[3,2048]{0,1:T(8,128)} %slice_bitcast_fusion.2, s32[4096]{0:T(1024)S(1)} %bitcast_clamp_fusion.1), kind=kCustom, calls=%fused_computation.1.clone | custom fusion | bytes 114688 | tf_op jit(solution)/shard_map/jit(_take)/gather | solution.py:70
  69.4 2.2 copy.82
  71.7 0.7 fusion.47
  72.3 0.1 fusion.49
  72.5 7.7 %all-to-all-start.1 = ((f32[3,32,128]{2,0,1:T(4,128)}), f32[3,32,128]{2,0,1:T(4,128)S(1)}, u32[]{:S(2)}, u32[]{:S(2)}) async-start(f32[3,32,128]{2,0,1:T(4,128)} %fusion.47), calls=%async_computation.1 | async-start | bytes 131072 | tf_op jit(solution)/shard_map/all_to_all | solution.py:127
  80.2 7.1 %all-to-all-done.1 = f32[3,32,128]{2,0,1:T(4,128)S(1)} async-done(((f32[3,32,128]{2,0,1:T(4,128)}), f32[3,32,128]{2,0,1:T(4,128)S(1)}, u32[]{:S(2)}, u32[]{:S(2)}) %all-to-all-start.1) | async-done | bytes 49184 | tf_op jit(solution)/shard_map/all_to_all | solution.py:127
  87.3 3.9 all-to-all-start.2
  91.2 10.1 %while.26 = (s32[]{:T(128)}, f32[3,2048]{1,0:T(4,128)S(1)}, s32[4096,1]{0,1:T(1,128)S(1)}, f32[3,4096]{1,0:T(4,128)S(1)}, s32[]{:T(128)}, /*index=5*/s32[]{:T(128)}, s32[]{:T(128)}, s32[]{:T(128)}) while((s32[]{:T(128)}, f32[3,2048]{1,0:T(4,128)S(1)}, s32[4096,1]{0,1:T(1,128)S(1)}, f32[3,4096]{1,0:T(4,128)S(1)}, s32[]{:T(128)}, ...), condition=%wide.region_6.9_spmd, body=%wide.region_5.8_spmd.sunk | while | flops 77595144 | bytes 94347 | solution.py:88
  91.3 2.5 fusion.76
  93.8 2.5 fusion.76
  96.3 2.5 fusion.76
  98.8 2.5 fusion.76
  101.3 1.3 copy.86
  102.7 98.0 %all-reduce = (f32[3,2048]{0,1:T(8,128)}, f32[3,2048]{0,1:T(8,128)}) all-reduce(f32[3,2048]{0,1:T(8,128)} %copy.86, f32[3,2048]{0,1:T(8,128)S(1)} %broadcast_select_fusion), channel_id=1, replica_groups=mesh['comp'=4,'tile'=32] {'comp'}, use_global_device_ids=true, to_apply=%region_7.10 | all-reduce | flops 12288 | bytes 98304 | tf_op jit(solution)/shard_map/psum | solution.py:135
  200.6 15.3 %gather_fusion.7 = f32[4096,3]{1,0:T(8,128)} fusion(f32[3,2048]{0,1:T(8,128)} %get-tuple-element.311, s32[4096]{0:T(1024)S(1)} %bitcast_clamp_fusion), kind=kCustom, calls=%fused_computation.7.clone | custom fusion | bytes 114688 | tf_op jit(solution)/shard_map/jit(_take)/gather | solution.py:70
  215.9 2.2 copy.89
  218.1 0.7 fusion.46
  218.8 7.9 %all-to-all-start.3 = ((f32[3,32,128]{2,0,1:T(4,128)}), f32[3,32,128]{2,0,1:T(4,128)S(1)}, u32[]{:S(2)}, u32[]{:S(2)}) async-start(f32[3,32,128]{2,0,1:T(4,128)} %fusion.46), calls=%async_computation.3 | async-start | bytes 131072 | tf_op jit(solution)/shard_map/all_to_all | solution.py:139
  226.7 7.1 %all-to-all-done.3 = f32[3,32,128]{2,0,1:T(4,128)S(1)} async-done(((f32[3,32,128]{2,0,1:T(4,128)}), f32[3,32,128]{2,0,1:T(4,128)S(1)}, u32[]{:S(2)}, u32[]{:S(2)}) %all-to-all-start.3) | async-done | bytes 49184 | tf_op jit(solution)/shard_map/all_to_all | solution.py:139
  233.8 10.1 %while.27 = (s32[]{:T(128)}, f32[3,2048]{1,0:T(4,128)S(1)}, s32[4096,1]{0,1:T(1,128)S(1)}, f32[3,4096]{1,0:T(4,128)S(1)}, s32[]{:T(128)}, /*index=5*/s32[]{:T(128)}, s32[]{:T(128)}, s32[]{:T(128)}) while((s32[]{:T(128)}, f32[3,2048]{1,0:T(4,128)S(1)}, s32[4096,1]{0,1:T(1,128)S(1)}, f32[3,4096]{1,0:T(4,128)S(1)}, s32[]{:T(128)}, ...), condition=%wide.region_10.13_spmd, body=%wide.region_9.12_spmd.sunk | while | flops 77595144 | bytes 94347 | solution.py:88
  233.8 2.5 fusion.79
  236.3 2.5 fusion.79
  238.9 2.5 fusion.79
  241.4 2.5 fusion.79
  243.9 0.4 copy.91
  244.3 1.3 collective-permute-start.1
  245.6 2.3 broadcast_select_fusion.1
  247.9 1.6 copy.92
  249.4 3.3 collective-permute-start.3
  252.7 0.7 collective-permute-done.3
  253.4 0.1 pad_maximum_fusion
  253.6 3.5 copy.70
  257.0 17.7 %gather_fusion.2 = f32[2048,3,64]{2,1,0:T(4,128)} fusion(f32[3,64,2304]{1,0,2:T(4,128)} %copy.70, s32[2048]{0:T(1024)S(1)} %fusion.53), kind=kCustom, calls=%fused_computation.3.clone | custom fusion | bytes 3153920 | tf_op jit(solution)/shard_map/jit(_take)/gather | solution.py:95
  274.7 17.6 %gather_fusion.3 = f32[2048,3,64]{2,1,0:T(4,128)} fusion(f32[3,64,2304]{1,0,2:T(4,128)} %copy.70, s32[2048]{0:T(1024)S(1)} %fusion.54), kind=kCustom, calls=%fused_computation.4.clone | custom fusion | bytes 3153920 | tf_op jit(solution)/shard_map/jit(_take)/gather | solution.py:95
  292.3 17.7 %gather_fusion.4 = f32[2048,3,64]{2,1,0:T(4,128)} fusion(f32[3,64,2304]{1,0,2:T(4,128)} %copy.70, s32[2048]{0:T(1024)S(1)} %fusion.55), kind=kCustom, calls=%fused_computation.5.clone | custom fusion | bytes 3153920 | tf_op jit(solution)/shard_map/jit(_take)/gather | solution.py:95
  310.1 17.6 %gather_fusion.5 = f32[2048,3,64]{2,1,0:T(4,128)} fusion(f32[3,64,2304]{1,0,2:T(4,128)} %copy.70, s32[2048]{0:T(1024)S(1)} %fusion.56), kind=kCustom, calls=%fused_computation.6.clone | custom fusion | bytes 3153920 | tf_op jit(solution)/shard_map/jit(_take)/gather | solution.py:95
  327.7 17.7 %gather_fusion = f32[2048,3,64]{2,1,0:T(4,128)} fusion(f32[3,64,2304]{1,0,2:T(4,128)} %copy.70, s32[2048]{0:T(1024)S(1)} %fusion.51), kind=kCustom, calls=%fused_computation.clone | custom fusion | bytes 3153920 | tf_op jit(solution)/shard_map/jit(_take)/gather | solution.py:95
  345.5 17.7 %gather_fusion.1 = f32[2048,3,64]{2,1,0:T(4,128)} fusion(f32[3,64,2304]{1,0,2:T(4,128)} %copy.70, s32[2048]{0:T(1024)S(1)} %fusion.52), kind=kCustom, calls=%fused_computation.2.clone | custom fusion | bytes 3153920 | tf_op jit(solution)/shard_map/jit(_take)/gather | solution.py:95
  363.1 31.5 %fusion.34 = f32[3,64,2048]{1,0,2:T(4,128)} fusion(f32[2048,3,64]{2,1,0:T(4,128)} %gather_fusion.5, f32[2048,3,64]{2,1,0:T(4,128)} %gather_fusion.4, f32[2048,3,64]{2,1,0:T(4,128)} %gather_fusion.3, f32[2048,3,64]{2,1,0:T(4,128)} %gather_fusion.2, f32[2048,3,64]{2,1,0:T(4,128)} %gather_fusion.1, f32[2048,3,64]{2,1,0:T(4,128)} %gather_fusion, ...), kind=kLoop, calls=%fused_computation.44 | loop fusion | flops 6684672 | bytes 11034624 | tf_op jit(solution)/shard_map/add | solution.py:96
  394.6 44.3 %conditional.3 = (f32[3,64,2048]{2,1,0:T(8,128)S(1)}, f32[3,64,2048]{0,2,1:T(8,128)}) conditional(s32[]{:T(128)} %convert_element_type.67, (f32[3,64,2048]{2,1,0:T(8,128)S(1)}, f32[3,64,2048]{1,0,2:T(4,128)}, f32[2048]{0:T(1024)S(1)}, f32[3,64,2048]{0,2,1:T(8,128)}) %tuple.53, (f32[2048]{0:T(1024)S(1)}, f32[2048]{0:T(1024)S(1)}, ...), branch_computations={%region_3.5_spmd, %region_4.6_spmd} | conditional | flops 1181696 | bytes 11042832 | solution.py:171
  394.7 39.2 %copy.78 = f32[3,64,2048]{2,1,0:T(8,128)} copy(f32[3,64,2048]{0,2,1:T(8,128)} %get-tuple-element.383) | data formatting | bytes 3145728 | tf_op jit(solution)/shard_map
  433.9 3.4 copy.79
  437.3 1.7 subtract_multiply_fusion
  439.0 38.4 %copy.97 = f32[3,64,2048]{2,1,0:T(8,128)S(1)} copy(f32[3,64,2048]{0,2,1:T(8,128)} %get-tuple-element.287) | data formatting | bytes 3145728 | tf_op jit(solution)/shard_map
  477.4 2.8 fusion.40
  (52 shorter events, 0.3 us)
Async XLA Ops:
  0.0 32.9 %copy-start.2 = (f32[1,1,3,64,2048]{4,3,2,1,0:T(8,128)S(1)}, f32[1,1,3,64,2048]{4,3,2,1,0:T(8,128)}, u32[]{:S(2)}) copy-start(f32[1,1,3,64,2048]{4,3,2,1,0:T(8,128)} %param.23) | copy-start | bytes 4718596
  0.0 32.9 %copy-start.7 = (f32[1,1,2048]{2,1,0:T(1,128)S(1)}, f32[1,1,2048]{2,1,0:T(1,128)}, u32[]{:S(2)}) copy-start(f32[1,1,2048]{2,1,0:T(1,128)} %param.24) | copy-start | bytes 24580
  32.9 0.7 copy-start.12
  33.0 8.5 %copy-start.8 = (s32[1,1,32,2,128]{4,3,2,1,0:T(2,128)S(1)}, s32[1,1,32,2,128]{4,3,2,1,0:T(2,128)}, u32[]{:S(2)}) copy-start(s32[1,1,32,2,128]{4,3,2,1,0:T(2,128)} %param.28) | copy-start | bytes 98308
  33.0 16.4 %copy-start.3 = (s32[1,1,6,2048]{3,1,2,0:T(1,128)S(1)}, s32[1,1,6,2048]{3,1,2,0:T(1,128)}, u32[]{:S(2)}) copy-start(s32[1,1,6,2048]{3,1,2,0:T(1,128)} %param.26) | copy-start | bytes 147460
  34.7 214.7 %collective-permute-start.2 = (f32[3,64,128]{2,1,0:T(8,128)S(1)}, f32[3,64,128]{2,1,0:T(8,128)S(1)}, u32[]{:S(2)}, u32[]{:S(2)}) collective-permute-start(f32[3,64,128]{2,1,0:T(8,128)S(1)} %get-tuple-element.317), channel_id=1, source_target_pairs={{1,0},{2,1},{3,2},{4,3},{5,4},{6,5},{7,6},{8,7},{9,8},{10,9},{11,1... | collective-permute-start | bytes 294920 | tf_op jit(solution)/shard_map/ppermute | solution.py:25
  41.5 202.8 %collective-permute-start = (f32[3,64,128]{2,1,0:T(8,128)S(1)}, f32[3,64,128]{2,1,0:T(8,128)S(1)}, u32[]{:S(2)}, u32[]{:S(2)}) collective-permute-start(f32[3,64,128]{2,1,0:T(8,128)S(1)} %get-tuple-element.316), channel_id=1, source_target_pairs={{0,1},{1,2},{2,3},{3,4},{4,5},{5,6},{6,7},{7,8},{8,9},{9,10},{10,1... | collective-permute-start | bytes 294920 | tf_op jit(solution)/shard_map/ppermute | solution.py:23
  42.1 30.4 %all-to-all-start = ((f32[1,32,128]{2,0,1:T(1,128)}), f32[1,32,128]{2,0,1:T(1,128)S(1)}, u32[]{:S(2)}, u32[]{:S(2)}) async-start(f32[1,32,128]{2,0,1:T(1,128)} %bitcast.26), calls=%async_computation | async-start | bytes 32768 | tf_op jit(solution)/shard_map/all_to_all | solution.py:128
  52.1 1.3 copy-start.9
  53.5 18.2 %copy-start.10 = (f32[1,1,32,128]{3,2,1,0:T(8,128)S(1)}, f32[1,1,32,128]{3,2,1,0:T(8,128)}, u32[]{:S(2)}) copy-start(f32[1,1,32,128]{3,2,1,0:T(8,128)} %param.29) | copy-start | bytes 49156
  53.5 18.9 %copy-start.6 = (f32[1,64,64]{2,1,0:T(8,128)S(1)}, f32[1,64,64]{2,1,0:T(8,128)}, u32[]{:S(2)}) copy-start(f32[1,64,64]{2,1,0:T(8,128)} %param.25) | copy-start | bytes 49156
  72.5 14.9 %all-to-all-start.1 = ((f32[3,32,128]{2,0,1:T(4,128)}), f32[3,32,128]{2,0,1:T(4,128)S(1)}, u32[]{:S(2)}, u32[]{:S(2)}) async-start(f32[3,32,128]{2,0,1:T(4,128)} %fusion.47), calls=%async_computation.1 | async-start | bytes 131072 | tf_op jit(solution)/shard_map/all_to_all | solution.py:127
  87.3 131.5 %all-to-all-start.2 = ((f32[1,32,128]{2,0,1:T(1,128)}), f32[1,32,128]{2,0,1:T(1,128)S(1)}, u32[]{:S(2)}, u32[]{:S(2)}) async-start(f32[1,32,128]{2,0,1:T(1,128)} %bitcast.38), calls=%async_computation.2 | async-start | bytes 32768 | tf_op jit(solution)/shard_map/all_to_all | solution.py:140
  200.6 17.5 %copy-start.11 = (f32[1,1,32,128]{3,2,1,0:T(8,128)S(1)}, f32[1,1,32,128]{3,2,1,0:T(8,128)}, u32[]{:S(2)}) copy-start(f32[1,1,32,128]{3,2,1,0:T(8,128)} %param.31) | copy-start | bytes 49156
  218.8 15.0 %all-to-all-start.3 = ((f32[3,32,128]{2,0,1:T(4,128)}), f32[3,32,128]{2,0,1:T(4,128)S(1)}, u32[]{:S(2)}, u32[]{:S(2)}) async-start(f32[3,32,128]{2,0,1:T(4,128)} %fusion.46), calls=%async_computation.3 | async-start | bytes 131072 | tf_op jit(solution)/shard_map/all_to_all | solution.py:139
  244.3 8.4 %collective-permute-start.1 = (f32[3,64,128]{2,1,0:T(8,128)S(1)}, f32[3,64,128]{2,1,0:T(8,128)S(1)}, u32[]{:S(2)}, u32[]{:S(2)}) collective-permute-start(f32[3,64,128]{2,1,0:T(8,128)S(1)} %collective-permute-done), channel_id=1, source_target_pairs={{0,32},{32,64},{64,96},{1,33},{33,65},{65,97},{2,34},{34,66},{66,9... | collective-permute-start | bytes 294920 | tf_op jit(solution)/shard_map/ppermute | solution.py:23
  249.4 4.0 collective-permute-start.3
where the time goes:
time: 483 us; the launch traced here: 480 us
  local copies, waits for them, and re-layouts  265 us (55%)
  blocking collectives  98 us (20%)
  other arithmetic  40.1 us (8%)
  starting transfers between devices  38.1 us (8%)
  matrix products  24 us (5%)
  waiting for transfers between devices  14.9 us (3%)
    gather x6, local copies, waits for them, and re-layouts, linked_rows(): picked = jnp.take(extended, jnp.maximum(index, 0), axis=2)  106 us
    psum x1, blocking collectives, per_device(): forcing_ocean, sea_all = lax.psum((partial_value, sea_part), 'comp')  98 us
    another operation x3, local copies, waits for them, and re-layouts  81 us
    gather x4, local copies, waits for them, and re-layouts, pack_rows(): picked = jnp.take(values, jnp.maximum(sources, 0), axis=1)  35 us
    unnamed x21, local copies, waits for them, and re-layouts  33.4 us
    add x1, other arithmetic, linked_rows(): total = total + jnp.where(index >= 0, picked, 0.0)  31.5 us
    dot_general x8, matrix products, land_block(): jnp.dot(rows, onehot, precision=lax.Precision.HIGHEST, preferred_element_...  20.1 us
    ppermute x2, starting transfers between devices, extended_2(): lax.ppermute(head, axis, [((i + 1) % count, i) for i in range(ends)])  10 us
  transfers between devices with their start and end apart: 8, of which 3 were waited for; matrix products, arithmetic and copies ran while one was open for 14% of the time, Pallas kernels for 0%

commit v1 on v0

v1 whole, which is shorter than its diff:
```python
import functools
import math

import jax
import jax.numpy as jnp
import numpy as np
from jax import lax
from jax.experimental import pallas as pl
from jax.experimental.pallas import tpu as pltpu
from jax.sharding import PartitionSpec as P

VISCOSITY = 0.05
ATM_STEP = 0.02
OCEAN_RATE = 0.08
COUPLING = 0.5
LANES = 128
BF = jnp.bfloat16
F32 = jnp.float32
VMEM_LIMIT = 48 * 1024 * 1024


def gll_matrix():
    points = np.array([-1.0, -1.0 / math.sqrt(5.0), 1.0 / math.sqrt(5.0), 1.0])
    legendre = 0.5 * (5.0 * points * points * points - 3.0 * points)
    matrix = np.zeros((4, 4))
    for a in range(4):
        for b in range(4):
            if a != b:
                matrix[a, b] = legendre[a] / (legendre[b] * (points[a] - points[b]))
    matrix[0, 0] = -3.0
    matrix[3, 3] = 3.0
    return matrix


def derivative_table():
    matrix = gll_matrix()
    along_xi = np.kron(np.eye(4), matrix)
    along_eta = np.kron(matrix, np.eye(4))
    second = along_xi @ along_xi + along_eta @ along_eta
    parts = [np.kron(np.eye(8), part).T for part in (along_xi, along_eta, second)]
    full = np.concatenate(parts, axis=1).astype(np.float32)
    high = full.astype(BF)
    low = (full - high.astype(np.float32)).astype(BF)
    return jnp.asarray(high), jnp.asarray(low)


def split(values):
    high = values.astype(BF)
    low = (values - high.astype(F32)).astype(BF)
    return high, low


def dot(a, b):
    return jnp.dot(a, b, preferred_element_type=F32)


def dot_nt(a, b):
    return lax.dot_general(a, b, (((1,), (1,)), ((), ())), preferred_element_type=F32)


def lane_pick(chunk_of, chunks, index):
    low = jnp.bitwise_and(index, LANES - 1)
    high = jnp.right_shift(index, 7)
    total = jnp.zeros(index.shape, F32)
    for at in range(chunks):
        row = jnp.broadcast_to(chunk_of(at), index.shape)
        picked = jnp.take_along_axis(row, low, axis=1, mode="promise_in_bounds")
        total = jnp.where(high == at, picked, total)
    return total


def out_kernel(flag, state, table, weight, payload):
    fields = state.shape[0]
    chunks = state.shape[2] // LANES

    @pl.when(flag[0] == 0)
    def _():
        source = table[:, 0, :]
        scale = weight[...]
        for f in range(fields):
            rows = lane_pick(lambda at: state[f, 0:1, at * LANES : (at + 1) * LANES], chunks, source)
            payload[:, f, :] = rows * scale
        payload[:, fields, :] = table[:, 1, :].astype(F32)

    @pl.when(flag[0] == 1)
    def _():
        payload[...] = jnp.zeros(payload.shape, F32)
        for f in range(fields):
            for at in range(chunks):
                payload[at, f : f + 1, :] = state[f, 0:1, at * LANES : (at + 1) * LANES]


def back_kernel(flag, got0, got1, got2, table, weight, payload):
    fields = got0.shape[1] - 1
    chunks = 16
    wide = fields + 1

    @pl.when(flag[0] == 0)
    def _():
        source = table[:, 0, :]
        scale = weight[...]
        for f in range(fields):
            pick = lambda at: got0[at, f : f + 1, :] + got1[at, f : f + 1, :] + got2[at, f : f + 1, :]
            rows = lane_pick(pick, chunks, source)
            payload[:, f, :] = rows * scale
        payload[:, fields, :] = table[:, 1, :].astype(F32)
        payload[:, wide:, :] = jnp.zeros((payload.shape[0], payload.shape[1] - wide, LANES), F32)

    @pl.when(flag[0] == 1)
    def _():
        payload[:, 0:wide, :] = got0[...]
        payload[:, wide : 2 * wide, :] = got1[...]
        payload[:, 2 * wide : 3 * wide, :] = got2[...]


def field_kernel(flag, state, metric, table_high, table_low, rims, high_ref, low_ref, left_ref, right_ref):
    rows, nodes = high_ref.shape
    third = rows // 3

    @pl.when(flag[0] == 0)
    def _():
        def chunk(at, carry):
            where = pl.ds(pl.multiple_of(at * LANES, LANES), LANES)
            values = state[:, where]
            high, low = split(values)
            both = dot(jnp.concatenate([high, low], axis=0), table_high[...])
            grads = both[:rows] + both[rows:] + dot(high, table_low[...])
            grad_xi = grads[:, :LANES]
            grad_eta = grads[:, LANES : 2 * LANES]
            second = grads[:, 2 * LANES :]
            scale = metric[0:1, where]
            wind_u = values[:third]
            wind_v = values[third : 2 * third]
            wind_u = jnp.concatenate([wind_u] * 3, axis=0)
            wind_v = jnp.concatenate([wind_v] * 3, axis=0)
            field = -scale * (wind_u * grad_xi + wind_v * grad_eta) + (VISCOSITY * scale * scale) * second
            fh, fl = split(field)
            high_ref[:, where] = fh
            low_ref[:, where] = fl
            return carry

        lax.fori_loop(0, nodes // LANES, chunk, 0)

    @pl.when(flag[0] == 1)
    def _():
        high, low = split(state[...])
        high_ref[...] = high
        low_ref[...] = low

    ids = lax.broadcasted_iota(jnp.int32, (nodes, LANES), 0)
    for side, target in ((0, left_ref), (1, right_ref)):
        onehot = jnp.where(ids == rims[side : side + 1, :], 1.0, 0.0).astype(BF)
        target[...] = dot(high_ref[...], onehot) + dot(low_ref[...], onehot)


def link_kernel(flag, high, low, left, right, state, metric, links, column, mixed, ext, count):
    rows, nodes = state.shape
    levels = column.shape[0]
    rim = left.shape[1]
    width = 2 * LANES
    blocks = (nodes + 2 * rim) // LANES
    lh, ll = split(left[...])
    rh, rl = split(right[...])
    ext[0:rows, 0:rim] = lh
    ext[rows:, 0:rim] = ll
    ext[0:rows, rim : rim + nodes] = high[...]
    ext[rows:, rim : rim + nodes] = low[...]
    ext[0:rows, rim + nodes :] = rh
    ext[rows:, rim + nodes :] = rl
    col_high, col_low = split(column[...])
    col = jnp.concatenate([col_high, col_low], axis=0)

    def run(rows_used, ocean):
        def tile(at, carry):
            where = pl.ds(pl.multiple_of(at * width, width), width)
            index = links[:, where]
            number = jnp.sum((index >= 0).astype(F32), axis=0, keepdims=True)
            lane_low = jnp.bitwise_and(index, LANES - 1)
            lane_high = jnp.right_shift(index, 7)
            ids = lax.broadcasted_iota(jnp.int32, (LANES, width), 0)
            lows = []
            highs = []
            for k in range(rows_used):
                lows.append(jnp.where(ids == lane_low[k : k + 1, :], 1.0, 0.0).astype(BF).reshape(8, 16, width))
                highs.append(jnp.broadcast_to(lane_high[k : k + 1, :], (16, width)).astype(BF))
            for block in range(blocks):
                total = None
                for k in range(rows_used):
                    mask = jnp.where(highs[k] == block, 1.0, 0.0).astype(BF)
                    term = lows[k] * mask[None]
                    total = term if total is None else total + term
                count[block * LANES : (block + 1) * LANES, :] = total.reshape(LANES, width)
            both = dot(ext[...], count[...])
            linked = both[:rows] + both[rows:]
            current = state[:, where]
            if ocean:
                gain = OCEAN_RATE * metric[0:1, where]
                updated = current + gain * (linked - number * current)
            else:
                gain = ATM_STEP / (1.0 + number)
                field = ext[0:rows, pl.ds(pl.multiple_of(at * width + rim, LANES), width)].astype(F32)
                field = field + ext[rows:, pl.ds(pl.multiple_of(at * width + rim, LANES), width)].astype(F32)
                updated = current + gain * (field + linked)
            uh, ul = split(updated)
            for f in range(rows // levels):
                part = slice(f * levels, (f + 1) * levels)
                full = dot(col, uh[part])
                mixed[part, where] = full[:levels] + full[levels:] + dot(col_high, ul[part])
            return carry

        lax.fori_loop(0, nodes // width, tile, 0)

    @pl.when(flag[0] == 0)
    def _():
        run(3, False)

    @pl.when(flag[0] == 1)
    def _():
        run(6, True)


def land_kernel(flag, got, mixed, column, result, left_rows, onehots):
    senders = got.shape[0]
    levels = column.shape[0]
    fields = 3
    chunks = 16
    ids = lax.broadcasted_iota(jnp.int32, (LANES, LANES), 0)
    ids_high = lax.broadcasted_iota(jnp.int32, (chunks, LANES), 0)

    def land(part, total):
        for a in range(senders):
            base = 4 * part
            cell = got[a, pl.ds(base + fields, 1), :].astype(jnp.int32)
            lane_low = jnp.bitwise_and(cell, LANES - 1)
            lane_high = jnp.right_shift(cell, 7)
            where = slice(a * LANES, (a + 1) * LANES)
            onehots[:, where] = jnp.where(ids == lane_low, 1.0, 0.0).astype(BF)
            mask = ids_high == lane_high
            picked = [jnp.where(mask, got[a, pl.ds(base + f, 1), :], 0.0) for f in range(fields)]
            high, low = split(jnp.concatenate(picked, axis=0))
            left_rows[0 : fields * chunks, where] = high
            left_rows[fields * chunks :, where] = low
        return total + dot_nt(left_rows[...], onehots[...])

    parts = jnp.where(flag[0] == 1, 3, 1)
    landed = lax.fori_loop(0, parts, land, jnp.zeros((2 * fields * chunks, LANES), F32))
    forcing = landed[: fields * chunks] + landed[fields * chunks :]
    gain = COUPLING * jnp.broadcast_to(column[:, 0:1], (levels, LANES))
    for f in range(fields):
        part = slice(f * levels, (f + 1) * levels)
        for at in range(chunks):
            where = slice(at * LANES, (at + 1) * LANES)
            result[part, where] = mixed[part, where] + gain * forcing[f * chunks + at : f * chunks + at + 1, :]


def call(kernel, flag, args, outs, scratch=(), specs=None):
    vmem = pl.BlockSpec(memory_space=pltpu.VMEM)
    specs = specs or [vmem] * len(args)
    return pl.pallas_call(
        kernel,
        in_specs=[pl.BlockSpec(memory_space=pltpu.SMEM)] + specs,
        out_specs=[vmem] * len(outs),
        out_shape=outs,
        scratch_shapes=list(scratch),
        compiler_params=pltpu.CompilerParams(vmem_limit_bytes=VMEM_LIMIT),
    )(flag, *args)


def per_device(state, metric, column_op, links, rims, out_map, out_weight, back_map, back_weight):
    _, _, fields, levels, nodes = state.shape
    rows = fields * levels
    rim = rims.shape[-1]
    ntile = lax.axis_size("tile")
    ncomp = lax.axis_size("comp")
    slot = out_map.shape[-1]
    both = ("comp", "tile")
    ocean_at = ncomp - 1
    total = ncomp * ntile
    edge = ocean_at * ntile - 1
    flag = (lax.axis_index("comp") == ocean_at).astype(jnp.int32).reshape(1)
    current = state.reshape(rows, nodes)
    metric_row = metric.reshape(1, nodes)
    column = column_op.reshape(levels, levels)
    vmem = pl.BlockSpec(memory_space=pltpu.VMEM)

    packed = jax.ShapeDtypeStruct((ntile, fields + 1, slot), F32)
    (payload,) = pl.pallas_call(
        out_kernel,
        grid=(1,),
        in_specs=[
            pl.BlockSpec(memory_space=pltpu.SMEM),
            pl.BlockSpec((fields, 8, nodes), lambda i: (0, 0, 0)),
            pl.BlockSpec((ntile, 2, slot), lambda i: (0, 0, 0)),
            pl.BlockSpec((ntile, slot), lambda i: (0, 0)),
        ],
        out_specs=[pl.BlockSpec((ntile, fields + 1, slot), lambda i: (0, 0, 0))],
        out_shape=[packed],
    )(flag, state.reshape(fields, levels, nodes), out_map.reshape(ntile, 2, slot), out_weight.reshape(ntile, slot))
    swapped = []
    for c in range(ocean_at):
        pairs = [(c * ntile + t, ocean_at * ntile + t) for t in range(ntile)]
        swapped.append(lax.ppermute(payload, both, pairs + [(b, a) for a, b in pairs]))

    table_high, table_low = derivative_table()
    half = jax.ShapeDtypeStruct((rows, nodes), BF)
    side = jax.ShapeDtypeStruct((rows, rim), F32)
    high, low, to_left, to_right = call(
        field_kernel,
        flag,
        (current, metric_row, table_high, table_low, rims.reshape(2, rim)),
        [half, half, side, side],
    )
    steps = [(i, i + 1) for i in range(total - 1) if i != edge]
    left = lax.ppermute(to_right, both, steps)
    right = lax.ppermute(to_left, both, [(b, a) for a, b in steps])

    (rows_out,) = call(
        back_kernel,
        flag,
        (*swapped, back_map.reshape(ntile, 2, slot), back_weight.reshape(ntile, slot)),
        [jax.ShapeDtypeStruct((ntile, ocean_at * (fields + 1), slot), F32)],
    )
    got = lax.all_to_all(rows_out, "tile", split_axis=0, concat_axis=0, tiled=True)

    full = jax.ShapeDtypeStruct((rows, nodes), F32)
    (mixed,) = call(
        link_kernel,
        flag,
        (high, low, left, right, current, metric_row, links.reshape(6, nodes), column),
        [full],
        [pltpu.VMEM((2 * rows, nodes + 2 * rim), BF), pltpu.VMEM((nodes + 2 * rim, 2 * LANES), BF)],
    )
    (result,) = call(
        land_kernel,
        flag,
        (got, mixed, column),
        [full],
        [pltpu.VMEM((2 * fields * (nodes // LANES), ntile * slot), BF), pltpu.VMEM((LANES, ntile * slot), BF)],
    )
    return result.reshape(state.shape)


def solution(mesh):
    return jax.shard_map(
        per_device,
        mesh=mesh,
        in_specs=(
            P("comp", "tile", None, None, None),
            P("comp", "tile", None),
            P("comp", None, None),
            P("comp", "tile", None, None),
            P("comp", "tile", None, None),
            P("comp", "tile", None, None, None),
            P("comp", "tile", None, None),
            P("comp", "tile", None, None, None),
            P("comp", "tile", None, None),
        ),
        out_specs=P("comp", "tile", None, None, None),
        check_vma=False,
    )
```

time: 483 us -> 53.4 us (0.11)
  the two profiles are of different devices: /device:TPU:17 before, /device:TPU:1 now
where the time goes in v1:
time: 53.4 us; the launch traced here: 52.9 us
  starting transfers between devices  27.6 us (52%)
  Pallas kernels  20.2 us (38%)
  waiting for transfers between devices  2.76 us (5%)
  local copies, waits for them, and re-layouts  2.19 us (4%)
    pallas_call x4, Pallas kernels, call(): pl.pallas_call(kernel, in_specs=[pl.BlockSpec(memory_space=pltpu.SMEM)] +...  17.8 us
    all_to_all x1, starting transfers between devices, per_device(): lax.all_to_all(rows_out, 'tile', split_axis=0, concat_axis=0, tiled=True)  9 us
    ppermute x3, starting transfers between devices, per_device(): lax.ppermute(payload, both, pairs + [(b, a) for a, b in pairs])  8.86 us
    ppermute x1, starting transfers between devices, per_device(): right = lax.ppermute(to_left, both, [(b, a) for a, b in steps])  6.64 us
    ppermute x1, starting transfers between devices, per_device(): left = lax.ppermute(to_right, both, steps)  3.14 us
    pallas_call x1, Pallas kernels, per_device(): pl.pallas_call(out_kernel, grid=(1,), in_specs=[pl.BlockSpec(memory_space...  2.37 us
    unnamed x19, local copies, waits for them, and re-layouts  2.19 us
    ppermute x1, waiting for transfers between devices, per_device(): left = lax.ppermute(to_right, both, steps)  1.3 us
  transfers between devices with their start and end apart: 6, of which 3 were waited for; matrix products, arithmetic and copies ran while one was open for 0% of the time, Pallas kernels for 27%

profile of v1, /device:TPU:1, one launch (start us, length us, event | category | flops | bytes accessed | tf_op | source)
XLA Modules:
  0.0 52.9 jit_solution(13086751135006267011)
XLA Ops:
  0.0 0.0 copy-start.2
  0.0 0.0 copy-start.3
  0.0 0.0 copy-start
  0.0 0.0 copy-start.4
  0.0 2.4 %shard_map.109 = f32[32,4,128]{2,1,0:T(4,128)} custom-call(s32[1]{0:T(128)} %bitcast.flag, f32[3,64,2048]{2,1,0:T(8,128)} %bitcast.14, s32[32,2,128]{2,1,0:T(2,128)} %bitcast.25, f32[32,128]{1,0:T(8,128)} %bitcast.26), custom_call_target="tpu_custom_call" | custom-call | tf_op jit(solution)/shard_map/pallas_call | solution.py:287
  2.4 0.0 copy-start.1
  2.4 0.8 %collective-permute-start = (f32[32,4,128]{2,1,0:T(4,128)}, f32[32,4,128]{2,1,0:T(4,128)S(1)}, u32[]{:S(2)}, u32[]{:S(2)}) collective-permute-start(f32[32,4,128]{2,1,0:T(4,128)} %shard_map.109), channel_id=1, source_target_pairs={{0,96},{1,97},{2,98},{3,99},{4,100},{5,101},{6,102},{7,103},{8,104... | collective-permute-start | bytes 196616 | tf_op jit(solution)/shard_map/ppermute | solution.py:302
  3.2 7.4 %collective-permute-start.1 = (f32[32,4,128]{2,1,0:T(4,128)}, f32[32,4,128]{2,1,0:T(4,128)S(1)}, u32[]{:S(2)}, u32[]{:S(2)}) collective-permute-start(f32[32,4,128]{2,1,0:T(4,128)} %shard_map.109), channel_id=1, source_target_pairs={{32,96},{33,97},{34,98},{35,99},{36,100},{37,101},{38,102},{39,103... | collective-permute-start | bytes 196616 | tf_op jit(solution)/shard_map/ppermute | solution.py:302
  10.6 0.7 %collective-permute-start.2 = (f32[32,4,128]{2,1,0:T(4,128)}, f32[32,4,128]{2,1,0:T(4,128)S(1)}, u32[]{:S(2)}, u32[]{:S(2)}) collective-permute-start(f32[32,4,128]{2,1,0:T(4,128)} %shard_map.109), channel_id=1, source_target_pairs={{64,96},{65,97},{66,98},{67,99},{68,100},{69,101},{70,102},{71,103... | collective-permute-start | bytes 196616 | tf_op jit(solution)/shard_map/ppermute | solution.py:302
  11.3 0.0 collective-permute-done.got0
  11.3 1.2 %collective-permute-done.1.got1 = f32[32,4,128]{2,1,0:T(4,128)S(1)} collective-permute-done((f32[32,4,128]{2,1,0:T(4,128)}, f32[32,4,128]{2,1,0:T(4,128)S(1)}, u32[]{:S(2)}, u32[]{:S(2)}) %collective-permute-start.1) | collective-permute-done | bytes 65568 | tf_op jit(solution)/shard_map/ppermute | solution.py:302
  12.5 0.0 collective-permute-done.2.got2
  12.5 0.0 copy-start.5
  12.5 0.8 %copy-done.5 = s32[1,1,32,2,128]{4,3,2,1,0:T(2,128)S(1)} copy-done((s32[1,1,32,2,128]{4,3,2,1,0:T(2,128)S(1)}, s32[1,1,32,2,128]{4,3,2,1,0:T(2,128)}, u32[]{:S(2)}) %copy-start.5) | copy-done | bytes 32792
  13.2 0.0 copy-start.6
  13.2 0.7 %copy-done.6 = f32[1,1,32,128]{3,2,1,0:T(8,128)S(1)} copy-done((f32[1,1,32,128]{3,2,1,0:T(8,128)S(1)}, f32[1,1,32,128]{3,2,1,0:T(8,128)}, u32[]{:S(2)}) %copy-start.6) | copy-done | bytes 16408
  13.9 0.0 copy-start.8
  13.9 1.4 %shard_map.110 = f32[32,12,128]{2,1,0:T(8,128)} custom-call(s32[1]{0:T(128)} %bitcast.flag, f32[32,4,128]{2,1,0:T(4,128)S(1)} %collective-permute-done.got0, f32[32,4,128]{2,1,0:T(4,128)S(1)} %collective-permute-done.1.got1, f32[32,4,128]{2,1,0:T(4,128)S(1)} %collective-permute-done.2.got2, s32[32,2,128]{2,1,0:T(2,128)S(1)} %bitcast.22, f32[32,128]{1,0:T(8,128)S(1)} %bitcast.23), custom_call_target="tpu_custom_call" | custom-call | tf_op jit(solution)/shard_map/pallas_call | solution.py:259
  15.4 9.0 %all-to-all-start = ((f32[32,12,128]{2,1,0:T(8,128)}), f32[32,12,128]{2,1,0:T(8,128)S(1)}, u32[]{:S(2)}, u32[]{:S(2)}) async-start(f32[32,12,128]{2,1,0:T(8,128)} %shard_map.110), calls=%async_computation | async-start | bytes 524288 | tf_op jit(solution)/shard_map/all_to_all | solution.py:323
  24.4 0.0 copy-done.2
  24.4 0.0 copy-done.3
  24.4 0.0 copy-done
  24.4 0.0 copy-done.4
  24.4 0.0 copy-start.7
  24.4 0.7 %copy-done.7 = s32[1,1,2,128]{3,2,1,0:T(2,128)S(1)} copy-done((s32[1,1,2,128]{3,2,1,0:T(2,128)S(1)}, s32[1,1,2,128]{3,2,1,0:T(2,128)}, u32[]{:S(2)}) %copy-start.7) | copy-done | bytes 1048
  25.1 5.6 %shard_map.111 = (bf16[192,2048]{1,0:T(8,128)(2,1)S(1)}, bf16[192,2048]{1,0:T(8,128)(2,1)S(1)}, f32[192,128]{1,0:T(8,128)S(1)}, f32[192,128]{1,0:T(8,128)S(1)}) custom-call(s32[1]{0:T(128)} %bitcast.flag, f32[192,2048]{1,0:T(8,128)S(1)} %bitcast.15, f32[1,2048]{1,0:T(1,128)S(1)} %bitcast.20, bf16[128,384]{1,0:T(8,128)(2,1)S(1)} %copy-done.2, ...), custom_call_target="tpu_custom_call" | custom-call | tf_op jit(solution)/shard_map/pallas_call | solution.py:259
  30.7 3.1 %collective-permute-start.3 = (f32[192,128]{1,0:T(8,128)S(1)}, f32[192,128]{1,0:T(8,128)S(1)}, u32[]{:S(2)}, u32[]{:S(2)}) collective-permute-start(f32[192,128]{1,0:T(8,128)S(1)} %get-tuple-element.11), channel_id=1, source_target_pairs={{0,1},{1,2},{2,3},{3,4},{4,5},{5,6},{6,7},{7,8},{8,9},{9,10},{10,1... | collective-permute-start | bytes 294920 | tf_op jit(solution)/shard_map/ppermute | solution.py:314
  33.8 6.6 %collective-permute-start.4 = (f32[192,128]{1,0:T(8,128)S(1)}, f32[192,128]{1,0:T(8,128)S(1)}, u32[]{:S(2)}, u32[]{:S(2)}) collective-permute-start(f32[192,128]{1,0:T(8,128)S(1)} %get-tuple-element.12), channel_id=1, source_target_pairs={{1,0},{2,1},{3,2},{4,3},{5,4},{6,5},{7,6},{8,7},{9,8},{10,9},{11,1... | collective-permute-start | bytes 294920 | tf_op jit(solution)/shard_map/ppermute | solution.py:315
  40.5 0.0 copy-done.8
  40.5 1.3 %collective-permute-done.3.left = f32[192,128]{1,0:T(8,128)S(1)} collective-permute-done((f32[192,128]{1,0:T(8,128)S(1)}, f32[192,128]{1,0:T(8,128)S(1)}, u32[]{:S(2)}, u32[]{:S(2)}) %collective-permute-start.3) | collective-permute-done | bytes 98336 | tf_op jit(solution)/shard_map/ppermute | solution.py:314
  41.8 0.3 collective-permute-done.4.right
  42.1 0.0 copy-done.1
  42.1 8.6 %shard_map.112.mixed = f32[192,2048]{1,0:T(8,128)S(1)} custom-call(s32[1]{0:T(128)} %bitcast.flag, bf16[192,2048]{1,0:T(8,128)(2,1)S(1)} %get-tuple-element.9.high, bf16[192,2048]{1,0:T(8,128)(2,1)S(1)} %get-tuple-element.10.low, f32[192,128]{1,0:T(8,128)S(1)} %collective-permute-done.3.left, f32[192,128]{1,0:T(8,128)S(1)} %collective-permute-done.4.right, ...), custom_call_target="tpu_custom_call" | custom-call | tf_op jit(solution)/shard_map/pallas_call | solution.py:259
  50.7 0.0 all-to-all-done.got
  50.7 2.2 %shard_map.113 = f32[192,2048]{1,0:T(8,128)} custom-call(s32[1]{0:T(128)} %bitcast.flag, f32[32,12,128]{2,1,0:T(8,128)S(1)} %all-to-all-done.got, f32[192,2048]{1,0:T(8,128)S(1)} %shard_map.112.mixed, f32[64,64]{1,0:T(8,128)S(1)} %bitcast.19), custom_call_target="tpu_custom_call" | custom-call | tf_op jit(solution)/shard_map/pallas_call | solution.py:259
  (1 shorter events, 0.0 us)
Async XLA Ops:
  0.0 24.4 %copy-start.2 = (bf16[128,384]{1,0:T(8,128)(2,1)S(1)}, bf16[128,384]{1,0:T(8,128)(2,1)}, u32[]{:S(2)}) copy-start(bf16[128,384]{1,0:T(8,128)(2,1)} %constant.12.clone.table_high) | copy-start | bytes 294916
  0.0 24.4 %copy-start.3 = (bf16[128,384]{1,0:T(8,128)(2,1)S(1)}, bf16[128,384]{1,0:T(8,128)(2,1)}, u32[]{:S(2)}) copy-start(bf16[128,384]{1,0:T(8,128)(2,1)} %constant.13.clone.table_low) | copy-start | bytes 294916
  0.0 24.4 %copy-start = (f32[1,1,3,64,2048]{4,3,2,1,0:T(8,128)S(1)}, f32[1,1,3,64,2048]{4,3,2,1,0:T(8,128)}, u32[]{:S(2)}) copy-start(f32[1,1,3,64,2048]{4,3,2,1,0:T(8,128)} %param.11) | copy-start | bytes 4718596
  0.0 24.4 %copy-start.4 = (f32[1,1,2048]{2,1,0:T(1,128)S(1)}, f32[1,1,2048]{2,1,0:T(1,128)}, u32[]{:S(2)}) copy-start(f32[1,1,2048]{2,1,0:T(1,128)} %param.12) | copy-start | bytes 24580
  2.4 39.7 %copy-start.1 = (f32[1,64,64]{2,1,0:T(8,128)S(1)}, f32[1,64,64]{2,1,0:T(8,128)}, u32[]{:S(2)}) copy-start(f32[1,64,64]{2,1,0:T(8,128)} %param.13) | copy-start | bytes 49156
  2.4 8.9 %collective-permute-start = (f32[32,4,128]{2,1,0:T(4,128)}, f32[32,4,128]{2,1,0:T(4,128)S(1)}, u32[]{:S(2)}, u32[]{:S(2)}) collective-permute-start(f32[32,4,128]{2,1,0:T(4,128)} %shard_map.109), channel_id=1, source_target_pairs={{0,96},{1,97},{2,98},{3,99},{4,100},{5,101},{6,102},{7,103},{8,104... | collective-permute-start | bytes 196616 | tf_op jit(solution)/shard_map/ppermute | solution.py:302
  3.2 9.3 %collective-permute-start.1 = (f32[32,4,128]{2,1,0:T(4,128)}, f32[32,4,128]{2,1,0:T(4,128)S(1)}, u32[]{:S(2)}, u32[]{:S(2)}) collective-permute-start(f32[32,4,128]{2,1,0:T(4,128)} %shard_map.109), channel_id=1, source_target_pairs={{32,96},{33,97},{34,98},{35,99},{36,100},{37,101},{38,102},{39,103... | collective-permute-start | bytes 196616 | tf_op jit(solution)/shard_map/ppermute | solution.py:302
  10.6 1.9 %collective-permute-start.2 = (f32[32,4,128]{2,1,0:T(4,128)}, f32[32,4,128]{2,1,0:T(4,128)S(1)}, u32[]{:S(2)}, u32[]{:S(2)}) collective-permute-start(f32[32,4,128]{2,1,0:T(4,128)} %shard_map.109), channel_id=1, source_target_pairs={{64,96},{65,97},{66,98},{67,99},{68,100},{69,101},{70,102},{71,103... | collective-permute-start | bytes 196616 | tf_op jit(solution)/shard_map/ppermute | solution.py:302
  12.5 0.8 %copy-start.5 = (s32[1,1,32,2,128]{4,3,2,1,0:T(2,128)S(1)}, s32[1,1,32,2,128]{4,3,2,1,0:T(2,128)}, u32[]{:S(2)}) copy-start(s32[1,1,32,2,128]{4,3,2,1,0:T(2,128)} %param.18) | copy-start | bytes 98308
  13.2 0.7 %copy-start.6 = (f32[1,1,32,128]{3,2,1,0:T(8,128)S(1)}, f32[1,1,32,128]{3,2,1,0:T(8,128)}, u32[]{:S(2)}) copy-start(f32[1,1,32,128]{3,2,1,0:T(8,128)} %param.19) | copy-start | bytes 49156
  13.9 26.5 %copy-start.8 = (s32[1,1,6,2048]{3,1,2,0:T(1,128)S(1)}, s32[1,1,6,2048]{3,1,2,0:T(1,128)}, u32[]{:S(2)}) copy-start(s32[1,1,6,2048]{3,1,2,0:T(1,128)} %param.14) | copy-start | bytes 147460
  15.4 35.3 %all-to-all-start = ((f32[32,12,128]{2,1,0:T(8,128)}), f32[32,12,128]{2,1,0:T(8,128)S(1)}, u32[]{:S(2)}, u32[]{:S(2)}) async-start(f32[32,12,128]{2,1,0:T(8,128)} %shard_map.110), calls=%async_computation | async-start | bytes 524288 | tf_op jit(solution)/shard_map/all_to_all | solution.py:323
  24.4 0.7 %copy-start.7 = (s32[1,1,2,128]{3,2,1,0:T(2,128)S(1)}, s32[1,1,2,128]{3,2,1,0:T(2,128)}, u32[]{:S(2)}) copy-start(s32[1,1,2,128]{3,2,1,0:T(2,128)} %param.15) | copy-start | bytes 3076
  30.7 11.1 %collective-permute-start.3 = (f32[192,128]{1,0:T(8,128)S(1)}, f32[192,128]{1,0:T(8,128)S(1)}, u32[]{:S(2)}, u32[]{:S(2)}) collective-permute-start(f32[192,128]{1,0:T(8,128)S(1)} %get-tuple-element.11), channel_id=1, source_target_pairs={{0,1},{1,2},{2,3},{3,4},{4,5},{5,6},{6,7},{7,8},{8,9},{9,10},{10,1... | collective-permute-start | bytes 294920 | tf_op jit(solution)/shard_map/ppermute | solution.py:314
  33.8 8.3 %collective-permute-start.4 = (f32[192,128]{1,0:T(8,128)S(1)}, f32[192,128]{1,0:T(8,128)S(1)}, u32[]{:S(2)}, u32[]{:S(2)}) collective-permute-start(f32[192,128]{1,0:T(8,128)S(1)} %get-tuple-element.12), channel_id=1, source_target_pairs={{1,0},{2,1},{3,2},{4,3},{5,4},{6,5},{7,6},{8,7},{9,8},{10,9},{11,1... | collective-permute-start | bytes 294920 | tf_op jit(solution)/shard_map/ppermute | solution.py:315

commit v2 on v1

v2 whole, which is shorter than its diff:
```python
import math

import jax
import jax.numpy as jnp
import numpy as np
from jax import lax
from jax.experimental import pallas as pl
from jax.experimental.pallas import tpu as pltpu
from jax.sharding import PartitionSpec as P

VISCOSITY = 0.05
ATM_STEP = 0.02
OCEAN_RATE = 0.08
COUPLING = 0.5
LANES = 128
BF = jnp.bfloat16
F32 = jnp.float32
MIB = 1024 * 1024
FINAL_LIMIT = 56


def gll_matrix():
    points = np.array([-1.0, -1.0 / math.sqrt(5.0), 1.0 / math.sqrt(5.0), 1.0])
    legendre = 0.5 * (5.0 * points * points * points - 3.0 * points)
    matrix = np.zeros((4, 4))
    for a in range(4):
        for b in range(4):
            if a != b:
                matrix[a, b] = legendre[a] / (legendre[b] * (points[a] - points[b]))
    matrix[0, 0] = -3.0
    matrix[3, 3] = 3.0
    return matrix


def derivative_table():
    matrix = gll_matrix()
    along_xi = np.kron(np.eye(4), matrix)
    along_eta = np.kron(matrix, np.eye(4))
    second = along_xi @ along_xi + along_eta @ along_eta
    parts = [np.kron(np.eye(8), part).T for part in (along_xi, along_eta, second)]
    full = np.concatenate(parts, axis=1).astype(np.float32)
    high = full.astype(BF)
    low = (full - high.astype(np.float32)).astype(BF)
    return jnp.asarray(np.concatenate([high, low], axis=0))


def split(values):
    high = values.astype(BF)
    low = (values - high.astype(F32)).astype(BF)
    return high, low


def dot(a, b):
    return jnp.dot(a, b, preferred_element_type=F32)


def dot_nt(a, b):
    return lax.dot_general(a, b, (((1,), (1,)), ((), ())), preferred_element_type=F32)


def lane_pick(chunk_of, chunks, index):
    low = jnp.bitwise_and(index, LANES - 1)
    high = jnp.right_shift(index, 7)
    total = jnp.zeros(index.shape, F32)
    for at in range(chunks):
        row = jnp.broadcast_to(chunk_of(at), index.shape)
        picked = jnp.take_along_axis(row, low, axis=1, mode="promise_in_bounds")
        total = jnp.where(high == at, picked, total)
    return total


def out_kernel(surface, table, weight, payload):
    atmos = lax.axis_index("comp") != lax.axis_size("comp") - 1
    fields = surface.shape[0]
    chunks = surface.shape[2] // LANES

    @pl.when(atmos)
    def _():
        source = table[:, 0, :]
        for f in range(fields):
            rows_of = lambda at: surface[f, 0:1, at * LANES : (at + 1) * LANES]
            payload[:, f, :] = lane_pick(rows_of, chunks, source) * weight[...]
        payload[:, fields, :] = table[:, 1, :].astype(F32)

    @pl.when(jnp.logical_not(atmos))
    def _():
        payload[...] = jnp.zeros(payload.shape, F32)
        for f in range(fields):
            for at in range(chunks):
                payload[at, f : f + 1, :] = surface[f, 0:1, at * LANES : (at + 1) * LANES]


def back_kernel(got0, got1, got2, table, weight, after, payload):
    comp = lax.axis_index("comp")
    fields = got0.shape[1] - 1
    chunks = 16
    wide = fields + 1

    @pl.when(comp != 3)
    def _():
        source = table[:, 0, :]
        scale = weight[...]
        for f in range(fields):

            def pick(at):
                first, second, third = (got[at, f : f + 1, :] for got in (got0, got1, got2))
                return jnp.where(comp == 0, first, jnp.where(comp == 1, second, third))

            rows = lane_pick(pick, chunks, source)
            payload[:, f, :] = rows * scale
        payload[:, fields, :] = table[:, 1, :].astype(F32)
        payload[:, wide:, :] = jnp.zeros((payload.shape[0], payload.shape[1] - wide, LANES), F32)

    @pl.when(comp == 3)
    def _():
        payload[:, 0:wide, :] = got0[...]
        payload[:, wide : 2 * wide, :] = got1[...]
        payload[:, 2 * wide : 3 * wide, :] = got2[...]


def pick_rims(wanted, parts):
    nodes = parts.shape[1]
    rows = parts.shape[0] // 2
    ids = lax.broadcasted_iota(jnp.int16, (nodes, LANES), 0)
    wanted = jnp.broadcast_to(wanted, (16, LANES)).astype(jnp.int16)
    wanted = jnp.broadcast_to(wanted[None], (nodes // 16, 16, LANES)).reshape(nodes, LANES)
    onehot = jnp.where(ids == wanted, jnp.ones((), BF), jnp.zeros((), BF))
    both = dot(parts[...], onehot)
    return both[:rows] + both[rows:]


def count_links(index, order, target):
    width = target.shape[1]
    one = jnp.ones((16, width), BF)
    zero = jnp.zeros((16, width), BF)
    ids = lax.broadcasted_iota(jnp.int16, (16, width), 0)
    low_off = [
        jnp.broadcast_to(jnp.bitwise_and(row, LANES - 1), (16, width)).astype(jnp.int16) - ids for row in index
    ]
    highs = [jnp.broadcast_to(jnp.right_shift(row, 7), (16, width)).astype(BF) for row in index]
    masks = [[jnp.where(high == block, one, zero) for high in highs] for block in order]
    for sub in range(LANES // 16):
        lows = [jnp.where(off == sub * 16, one, zero) for off in low_off]
        for slot in range(len(order)):
            total = None
            for low, mask in zip(lows, masks[slot]):
                term = low * mask
                total = term if total is None else total + term
            target[slot * LANES + sub * 16 : slot * LANES + sub * 16 + 16, :] = total

def gain_of(ocean, number, metric):
    return OCEAN_RATE * metric if ocean else ATM_STEP / (1.0 + number)

def atmos_field(values, scale, table_high, table_low):
    third = values.shape[0] // 3
    high, low = split(values)
    grads = dot(high, table_high) + dot(low, table_high) + dot(high, table_low)
    grad_xi = grads[:, :LANES]
    grad_eta = grads[:, LANES : 2 * LANES]
    second = grads[:, 2 * LANES :]
    wind_u = jnp.concatenate([values[:third]] * 3, axis=0)
    wind_v = jnp.concatenate([values[third : 2 * third]] * 3, axis=0)
    return (VISCOSITY * scale * scale) * second - scale * (wind_u * grad_xi + wind_v * grad_eta)


def field_kernel(state, metric, tables, rims, after, parts, left_ref, right_ref):
    atmos = lax.axis_index("comp") != lax.axis_size("comp") - 1
    rows, nodes = state.shape

    @pl.when(atmos)
    def _():
        for at in range(nodes // LANES):
            where = slice(at * LANES, (at + 1) * LANES)
            field = atmos_field(state[:, where], metric[0:1, where], tables[:LANES, :], tables[LANES:, :])
            high, low = split(field)
            parts[0:rows, where] = high
            parts[rows:, where] = low

    @pl.when(jnp.logical_not(atmos))
    def _():
        high, low = split(state[...])
        parts[0:rows, :] = high
        parts[rows:, :] = low

    left_ref[...] = pick_rims(rims[0:1, :], parts)
    right_ref[...] = pick_rims(rims[1:2, :], parts)


def inner_kernel(parts, state, metric, links, after, partial, count):
    atmos = lax.axis_index("comp") != lax.axis_size("comp") - 1
    rows, nodes = state.shape
    unroll, _, width = count.shape
    chunks = nodes // LANES
    def run(used, is_ocean):
        def step(at, here):
            where = pl.ds(pl.multiple_of(at * width, width), width)
            index = [links[k, :, where] for k in range(used)]
            number = sum((row >= 0).astype(F32) for row in index)
            count_links(index, list(range(1, chunks + 1)), here)
            both = dot(parts[...], here[...])
            linked = both[:rows] + both[rows:]
            current = state[:, where]
            gain = gain_of(is_ocean, number, metric[0:1, where])
            if is_ocean:
                partial[:, where] = current + gain * (linked - number * current)
            else:
                field = parts[0:rows, where].astype(F32) + parts[rows:, where].astype(F32)
                partial[:, where] = current + gain * (field + linked)

        def group(i, carry):
            for u in range(unroll):
                step(i * unroll + u, count.at[u])
            return carry

        lax.fori_loop(0, nodes // width // unroll, group, 0)

    @pl.when(atmos)
    def _():
        run(3, False)

    @pl.when(jnp.logical_not(atmos))
    def _():
        run(6, True)


def count_links(index, order, target):
    width = target.shape[1]
    one = jnp.ones((16, width), BF)
    zero = jnp.zeros((16, width), BF)
    ids = lax.broadcasted_iota(jnp.int16, (16, width), 0)
    low_off = [
        jnp.broadcast_to(jnp.bitwise_and(row, LANES - 1), (16, width)).astype(jnp.int16) - ids for row in index
    ]
    highs = [jnp.broadcast_to(jnp.right_shift(row, 7), (16, width)).astype(BF) for row in index]
    masks = [[jnp.where(high == block, one, zero) for high in highs] for block in order]
    for sub in range(LANES // 16):
        lows = [jnp.where(off == sub * 16, one, zero) for off in low_off]
        for slot in range(len(order)):
            total = None
            for low, mask in zip(lows, masks[slot]):
                term = low * mask
                total = term if total is None else total + term
            target[slot * LANES + sub * 16 : slot * LANES + sub * 16 + 16, :] = total

def gain_of(ocean, number, metric):
    return OCEAN_RATE * metric if ocean else ATM_STEP / (1.0 + number)

def rims_there(left, right, token):
    token[...] = jnp.zeros(token.shape, F32)


def final_kernel(
    partial_in, left_in, right_in, got_in, metric_in, links_in, column_in, after, result,
    partial, sides, got, metric, links, column, done, rim_parts, count, left_rows, onehots, sems,
):
    comp = lax.axis_index("comp")
    tile = lax.axis_index("tile")
    last_comp = lax.axis_size("comp") - 1
    last_tile = lax.axis_size("tile") - 1
    ocean = comp == last_comp
    atmos = jnp.logical_not(ocean)
    has_left = jnp.logical_not((tile == 0) & (ocean | (comp == 0)))
    has_right = jnp.logical_not((tile == last_tile) & (comp >= last_comp - 1))
    rows, nodes = partial.shape
    levels = column.shape[0]
    senders = got.shape[0]
    rim = left_in.shape[1]
    unroll, _, width = count.shape
    tiles = nodes // width
    fields = rows // levels
    chunks = nodes // LANES
    columns = [pl.ds(n * width, width) for n in range(tiles)]
    moves = [(got_in, got), (links_in, links), (left_in, sides.at[0]), (right_in, sides.at[1])]
    moves += [(metric_in, metric), (column_in, column)]
    moves += [(partial_in.at[:, where], partial.at[:, where]) for where in columns]
    copies = [pltpu.make_async_copy(a, b, sems.at[n]) for n, (a, b) in enumerate(moves)]
    for copy in copies:
        copy.start()
    copies[0].wait()
    ids = lax.broadcasted_iota(jnp.int32, (LANES, LANES), 0)
    ids_high = lax.broadcasted_iota(jnp.int32, (chunks, LANES), 0)

    def land(part, total):
        for a in range(senders):
            base = 4 * part
            cell = got[a, pl.ds(base + fields, 1), :].astype(jnp.int32)
            lane_low = jnp.bitwise_and(cell, LANES - 1)
            lane_high = jnp.right_shift(cell, 7)
            where = slice(a * LANES, (a + 1) * LANES)
            onehots[:, where] = jnp.where(ids == lane_low, 1.0, 0.0).astype(BF)
            mask = ids_high == lane_high
            picked = [jnp.where(mask, got[a, pl.ds(base + f, 1), :], 0.0) for f in range(fields)]
            high, low = split(jnp.concatenate(picked, axis=0))
            left_rows[0 : fields * chunks, where] = high
            left_rows[fields * chunks :, where] = low
        return total + dot_nt(left_rows[...], onehots[...])

    groups = jnp.where(ocean, last_comp, 1)
    landed = lax.fori_loop(0, groups, land, jnp.zeros((2 * fields * chunks, LANES), F32))
    forcing = COUPLING * (landed[: fields * chunks] + landed[fields * chunks :])

    for copy in copies[1:6]:
        copy.wait()
    for side, there in ((0, has_left), (1, has_right)):
        high, low = split(jnp.where(there, sides[side], 0.0))
        rim_parts[0:rows, side * rim : (side + 1) * rim] = high
        rim_parts[rows:, side * rim : (side + 1) * rim] = low
    col_high, col_low = split(column[...])
    col_gain = column[:, 0:1]
    col = jnp.concatenate([col_high, col_low], axis=0)

    def move(at):
        return pltpu.make_async_copy(done.at[:, columns[at]], result.at[:, columns[at]], sems.at[6 + tiles + at])

    def run(used, is_ocean):
        for at in range(tiles):
            where = slice(at * width, (at + 1) * width)
            here = count.at[at % unroll]
            index = [links[k, :, where] for k in range(used)]
            number = sum((row >= 0).astype(F32) for row in index)
            count_links(index, [0, chunks + 1], here)
            both = dot(rim_parts[...], here[...])
            gain = gain_of(is_ocean, number, metric[0:1, where])
            copies[6 + at].wait()
            updated = partial[:, where] + gain * (both[:rows] + both[rows:])
            uh, ul = split(updated)
            for f in range(fields):
                part = slice(f * levels, (f + 1) * levels)
                full = dot(col, uh[part])
                mixed = full[:levels] + full[levels:] + dot(col_high, ul[part])
                first = f * chunks + at * width // LANES
                rows_of = [forcing[n : n + 1, :] for n in range(first, first + width // LANES)]
                done[part, where] = mixed + col_gain * jnp.concatenate(rows_of, axis=1)
            move(at).start()

    @pl.when(atmos)
    def _():
        run(3, False)

    @pl.when(ocean)
    def _():
        run(6, True)

    for at in range(tiles):
        move(at).wait()


def call(kernel, args, outs, scratch=(), limit=32, form="vmem", anywhere=(), cost=None):
    free = pl.BlockSpec(memory_space=pl.ANY)
    whole = pl.BlockSpec(memory_space=pltpu.VMEM)

    def spec(dims):
        if form == "block":
            return pl.BlockSpec(dims, lambda i: (0,) * len(dims))
        return free if form == "any" else whole

    params = pltpu.CompilerParams() if limit is None else pltpu.CompilerParams(vmem_limit_bytes=limit * MIB)
    return pl.pallas_call(
        kernel,
        grid=(1,) if form == "block" else (),
        in_specs=[free if n in anywhere else spec(arg.shape) for n, arg in enumerate(args)],
        out_specs=[spec(out.shape) for out in outs],
        out_shape=outs,
        scratch_shapes=list(scratch),
        compiler_params=params,
        cost_estimate=cost and pl.CostEstimate(flops=cost, bytes_accessed=4_000_000, transcendentals=0),
    )(*args)


def per_device(state, metric, column_op, links, rims, out_map, out_weight, back_map, back_weight):
    _, _, fields, levels, nodes = state.shape
    rows = fields * levels
    rim = rims.shape[-1]
    ntile = lax.axis_size("tile")
    ncomp = lax.axis_size("comp")
    slot = out_map.shape[-1]
    axes = ("comp", "tile")
    total = ncomp * ntile
    chunks = nodes // LANES
    width = 2 * LANES
    tiles = nodes // width
    metric_row = metric.reshape(1, nodes)
    link_rows = links.reshape(6, 1, nodes)
    tables = derivative_table()
    dma = pltpu.SemaphoreType.DMA
    int32 = jnp.int32

    def shape(*dims, kind=F32):
        return jax.ShapeDtypeStruct(dims, kind)

    def held(*dims, kind=F32):
        return pltpu.VMEM(dims, kind)

    (payload,) = pl.pallas_call(
        out_kernel,
        grid=(1,),
        in_specs=[
            pl.BlockSpec((fields, 8, nodes), lambda i: (0, 0, 0)),
            pl.BlockSpec((ntile, 2, slot), lambda i: (0, 0, 0)),
            pl.BlockSpec((ntile, slot), lambda i: (0, 0)),
        ],
        out_specs=[pl.BlockSpec((ntile, fields + 1, slot), lambda i: (0, 0, 0))],
        out_shape=[shape(ntile, fields + 1, slot)],
    )(state.reshape(fields, levels, nodes), out_map.reshape(ntile, 2, slot), out_weight.reshape(ntile, slot))

    def across(values, flip):
        pairs = [(a * ntile + b, (a ^ flip) * ntile + b) for a in range(ncomp) for b in range(ntile)]
        return lax.ppermute(values, axes, pairs)

    got1 = across(payload, 2)
    got2 = across(payload, 1)
    got0 = across(got1, 1)

    current = state.reshape(rows, nodes)
    parts, to_left, to_right = call(
        field_kernel,
        (current, metric_row, tables, rims.reshape(2, rim), payload),
        [shape(2 * rows, nodes, kind=BF), shape(rows, rim), shape(rows, rim)],
        anywhere=(4,),
        cost=4_000_000_000,
    )
    steps = [(i, (i + 1) % total) for i in range(total)]
    left = lax.ppermute(to_right, axes, steps)
    right = lax.ppermute(to_left, axes, [(b, a) for a, b in steps])
    (rows_out,) = call(
        back_kernel,
        (got0, got1, got2, back_map.reshape(ntile, 2, slot), back_weight.reshape(ntile, slot), to_left),
        [shape(ntile, (ncomp - 1) * (fields + 1), slot)],
        anywhere=(5,),
    )
    got = lax.all_to_all(rows_out, "tile", split_axis=0, concat_axis=0, tiled=True)

    (partial,) = call(
        inner_kernel,
        (parts, current, metric_row, link_rows, rows_out),
        [shape(rows, nodes)],
        [held(2, nodes, width, kind=BF)],
        anywhere=(4,),
        cost=8_000_000_000,
    )

    (rims_token,) = call(rims_there, (left, right), [shape(8, LANES)], anywhere=(0, 1), cost=8_000_000_000)
    (result,) = call(
        final_kernel,
        (partial, left, right, got, metric_row, link_rows, column_op.reshape(levels, levels), rims_token),
        [shape(rows, nodes)],
        [
            held(rows, nodes),
            held(2, rows, rim),
            held(ntile, (ncomp - 1) * (fields + 1), slot),
            held(1, nodes),
            held(6, 1, nodes, kind=int32),
            held(levels, levels),
            held(rows, nodes),
            held(2 * rows, 2 * rim, kind=BF),
            held(2, 2 * rim, width, kind=BF),
            held(2 * fields * chunks, ntile * slot, kind=BF),
            held(LANES, ntile * slot, kind=BF),
            dma((6 + 2 * tiles,)),
        ],
        limit=FINAL_LIMIT,
        form="any",
    )
    return result.reshape(state.shape)


def solution(mesh):
    return jax.shard_map(
        per_device,
        mesh=mesh,
        in_specs=(
            P("comp", "tile", None, None, None),
            P("comp", "tile", None),
            P("comp", None, None),
            P("comp", "tile", None, None),
            P("comp", "tile", None, None),
            P("comp", "tile", None, None, None),
            P("comp", "tile", None, None),
            P("comp", "tile", None, None, None),
            P("comp", "tile", None, None),
        ),
        out_specs=P("comp", "tile", None, None, None),
        check_vma=False,
    )
```

time: 53.4 us -> 43.9 us (0.82)
  starting transfers between devices: 27.6 us -> 16.6 us
  Pallas kernels: 20.2 us -> 16.9 us
  waiting for transfers between devices: 2.76 us -> 5.75 us
  local copies, waits for them, and re-layouts: 2.19 us -> 4.21 us
    ppermute x5, starting transfers between devices: 18.6 us -> 11.9 us  [the longest x1 6.34 us: per_device(): right = lax.ppermute(to_left, axes, [(b, a) for a, b in steps])]
    all_to_all x1, starting transfers between devices: 9 us -> 4.62 us  [per_device(): lax.all_to_all(rows_out, 'tile', split_axis=0, concat_axis=0, tiled=True)]
    pallas_call x5 -> x6, Pallas kernels: 20.2 us -> 16.9 us  [the longest x5 14.5 us: call(): pl.pallas_call(kernel, grid=(1,) if form == 'block' else (), in_specs=[fr...]
    all_to_all x1, waiting for transfers between devices: 0.01 us -> 2.95 us  [per_device(): lax.all_to_all(rows_out, 'tile', split_axis=0, concat_axis=0, tiled=True)]
    unnamed x19 -> x24, local copies, waits for them, and re-layouts: 2.19 us -> 4.21 us
  transfers between devices with their start and end apart: 6 -> 6, of which waited for: 3 -> 2; matrix products, arithmetic and copies ran while one was open for 0% -> 0% of each run, Pallas kernels for 27% -> 10%
where the time goes in v2:
time: 43.9 us; the launch traced here: 43.5 us
  Pallas kernels  16.9 us (38%)
  starting transfers between devices  16.6 us (38%)
  waiting for transfers between devices  5.75 us (13%)
  local copies, waits for them, and re-layouts  4.21 us (10%)
    pallas_call x5, Pallas kernels, call(): pl.pallas_call(kernel, grid=(1,) if form == 'block' else (), in_specs=[fr...  14.5 us
    ppermute x1, starting transfers between devices, per_device(): right = lax.ppermute(to_left, axes, [(b, a) for a, b in steps])  6.34 us
    all_to_all x1, starting transfers between devices, per_device(): lax.all_to_all(rows_out, 'tile', split_axis=0, concat_axis=0, tiled=True)  4.62 us
    unnamed x24, local copies, waits for them, and re-layouts  4.21 us
    ppermute x3, starting transfers between devices, across(): return lax.ppermute(values, axes, pairs)  3.4 us
    all_to_all x1, waiting for transfers between devices, per_device(): lax.all_to_all(rows_out, 'tile', split_axis=0, concat_axis=0, tiled=True)  2.95 us
    ppermute x3, waiting for transfers between devices, across(): return lax.ppermute(values, axes, pairs)  2.8 us
    pallas_call x1, Pallas kernels, per_device(): pl.pallas_call(out_kernel, grid=(1,), in_specs=[pl.BlockSpec((fields, 8,...  2.36 us
  transfers between devices with their start and end apart: 6, of which 2 were waited for; matrix products, arithmetic and copies ran while one was open for 0% of the time, Pallas kernels for 10%

profile of v2, /device:TPU:1, one launch (start us, length us, event | category | flops | bytes accessed | tf_op | source)
XLA Modules:
  0.0 43.5 jit_solution(2592148729639635881)
XLA Ops:
  0.0 0.0 copy-start
  0.0 0.0 copy-start.10
  0.0 0.0 copy-start.8
  0.0 2.4 %shard_map.100.after = f32[32,4,128]{2,1,0:T(4,128)} custom-call(f32[3,64,2048]{2,1,0:T(8,128)} %bitcast.11, s32[32,2,128]{2,1,0:T(2,128)} %bitcast.23, f32[32,128]{1,0:T(8,128)} %bitcast.24), custom_call_target="tpu_custom_call" | custom-call | tf_op jit(solution)/shard_map/pallas_call | solution.py:394
  2.4 0.0 copy-done
  2.4 0.0 copy-done.10
  2.4 0.0 copy-done.8
  2.4 0.0 copy-start.4
  2.4 0.8 %copy-done.4 = f32[32,4,128]{2,1,0:T(4,128)S(1)} copy-done((f32[32,4,128]{2,1,0:T(4,128)S(1)}, f32[32,4,128]{2,1,0:T(4,128)}, u32[]{:S(2)}) %copy-start.4) | copy-done | bytes 65560
  3.2 0.0 copy-start.11
  3.2 0.9 %copy-done.11 = bf16[256,384]{1,0:T(8,128)(2,1)S(1)} copy-done((bf16[256,384]{1,0:T(8,128)(2,1)S(1)}, bf16[256,384]{1,0:T(8,128)(2,1)}, u32[]{:S(2)}) %copy-start.11) | copy-done | bytes 196632
  4.1 3.0 %shard_map.101 = (bf16[384,2048]{1,0:T(8,128)(2,1)S(1)}, f32[192,128]{1,0:T(8,128)S(1)}, f32[192,128]{1,0:T(8,128)S(1)}) custom-call(f32[192,2048]{1,0:T(8,128)S(1)} %bitcast.12, f32[1,2048]{1,0:T(1,128)S(1)} %bitcast.19, bf16[256,384]{1,0:T(8,128)(2,1)S(1)} %copy-done.11, s32[2,128]{1,0:T(2,128)S(1)} %bitcast.21, f32[32,4,128]{2,1,0:T(4,128)S(1)} %copy-done.4), custom_call_target="tpu_custom_call" | custom-call | flops 4000000000 | bytes 4000000 | tf_op jit(solution)/shard_map/pallas_call | solution.py:358
  7.2 2.2 %collective-permute-start.3 = (f32[192,128]{1,0:T(8,128)S(1)}, f32[192,128]{1,0:T(8,128)S(1)}, u32[]{:S(2)}, u32[]{:S(2)}) collective-permute-start(f32[192,128]{1,0:T(8,128)S(1)} %get-tuple-element.10), channel_id=1, source_target_pairs={{0,1},{1,2},{2,3},{3,4},{4,5},{5,6},{6,7},{7,8},{8,9},{9,10},{10,1... | collective-permute-start | bytes 294920 | tf_op jit(solution)/shard_map/ppermute | solution.py:423
  9.4 0.0 copy-start.6
  9.4 0.0 copy-start.7
  9.4 0.0 copy-start.5
  9.4 6.3 %collective-permute-start.4 = (f32[192,128]{1,0:T(8,128)S(1)}, f32[192,128]{1,0:T(8,128)S(1)}, u32[]{:S(2)}, u32[]{:S(2)}) collective-permute-start(f32[192,128]{1,0:T(8,128)S(1)} %get-tuple-element.9.after), channel_id=1, source_target_pairs={{1,0},{2,1},{3,2},{4,3},{5,4},{6,5},{7,6},{8,7},{9,8},{10,9},{11,1... | collective-permute-start | bytes 294920 | tf_op jit(solution)/shard_map/ppermute | solution.py:424
  15.7 2.6 %collective-permute-start = (f32[32,4,128]{2,1,0:T(4,128)S(1)}, f32[32,4,128]{2,1,0:T(4,128)S(1)}, u32[]{:S(2)}, u32[]{:S(2)}) collective-permute-start(f32[32,4,128]{2,1,0:T(4,128)S(1)} %copy-done.4), channel_id=1, source_target_pairs={{0,64},{1,65},{2,66},{3,67},{4,68},{5,69},{6,70},{7,71},{8,72},{9,... | collective-permute-start | bytes 196616 | tf_op jit(solution)/shard_map/ppermute | solution.py:408
  18.3 0.0 collective-permute-start.2
  18.3 2.8 %collective-permute-done.got1 = f32[32,4,128]{2,1,0:T(4,128)S(1)} collective-permute-done((f32[32,4,128]{2,1,0:T(4,128)S(1)}, f32[32,4,128]{2,1,0:T(4,128)S(1)}, u32[]{:S(2)}, u32[]{:S(2)}) %collective-permute-start) | collective-permute-done | bytes 65568 | tf_op jit(solution)/shard_map/ppermute | solution.py:408
  21.1 0.8 %collective-permute-start.1 = (f32[32,4,128]{2,1,0:T(4,128)S(1)}, f32[32,4,128]{2,1,0:T(4,128)S(1)}, u32[]{:S(2)}, u32[]{:S(2)}) collective-permute-start(f32[32,4,128]{2,1,0:T(4,128)S(1)} %collective-permute-done.got1), channel_id=1, source_target_pairs={{0,32},{1,33},{2,34},{3,35},{4,36},{5,37},{6,38},{7,39},{8,40},{9,... | collective-permute-start | bytes 196616 | tf_op jit(solution)/shard_map/ppermute | solution.py:408
  21.9 0.0 collective-permute-done.3.left.left_in
  21.9 0.0 copy-start.2
  21.9 0.0 collective-permute-done.4.right.right_in
  21.9 0.0 copy-start.3
  21.9 0.6 %copy-done.2 = f32[192,128]{1,0:T(8,128)} copy-done((f32[192,128]{1,0:T(8,128)}, f32[192,128]{1,0:T(8,128)S(1)}, u32[]{:S(2)}) %copy-start.2) | copy-done | bytes 98328
  22.5 0.1 copy-done.3
  22.6 0.0 copy-start.9
  22.6 0.6 %copy-done.9 = f32[8,128]{1,0:T(8,128)} copy-done((f32[8,128]{1,0:T(8,128)}, f32[8,128]{1,0:T(8,128)S(1)}, u32[]{:S(2)}) %copy-start.9) | copy-done | bytes 4120
  23.2 0.0 collective-permute-done.2.got2
  23.2 0.0 collective-permute-done.1.got0
  23.2 0.0 copy-done.6
  23.2 0.0 copy-done.7
  23.2 1.4 %shard_map.102.after = f32[32,12,128]{2,1,0:T(8,128)} custom-call(f32[32,4,128]{2,1,0:T(4,128)S(1)} %collective-permute-done.1.got0, f32[32,4,128]{2,1,0:T(4,128)S(1)} %collective-permute-done.got1, f32[32,4,128]{2,1,0:T(4,128)S(1)} %collective-permute-done.2.got2, s32[32,2,128]{2,1,0:T(2,128)S(1)} %bitcast.16, f32[32,128]{1,0:T(8,128)S(1)} %bitcast.17, ...), custom_call_target="tpu_custom_call" | custom-call | tf_op jit(solution)/shard_map/pallas_call | solution.py:358
  24.7 4.6 %all-to-all-start = ((f32[32,12,128]{2,1,0:T(8,128)}), f32[32,12,128]{2,1,0:T(8,128)}, u32[]{:S(2)}, u32[]{:S(2)}) async-start(f32[32,12,128]{2,1,0:T(8,128)} %shard_map.102.after), calls=%async_computation | async-start | bytes 524288 | tf_op jit(solution)/shard_map/all_to_all | solution.py:431
  29.3 0.0 copy-done.5
  29.3 4.4 %shard_map.103.partial_in = f32[192,2048]{1,0:T(8,128)S(1)} custom-call(bf16[384,2048]{1,0:T(8,128)(2,1)S(1)} %get-tuple-element.8.parts, f32[192,2048]{1,0:T(8,128)S(1)} %bitcast.13, f32[1,2048]{1,0:T(1,128)S(1)} %bitcast.20, s32[6,1,2048]{2,1,0:T(1,128)S(1)} %bitcast.15, f32[32,12,128]{2,1,0:T(8,128)} %shard_map.102.after), custom_call_target="tpu_custom_call" | custom-call | flops 8000000000 | bytes 4000000 | tf_op jit(solution)/shard_map/pallas_call | solution.py:358
  33.7 0.0 copy-start.1
  33.7 1.2 %copy-done.1 = f32[192,2048]{1,0:T(8,128)} copy-done((f32[192,2048]{1,0:T(8,128)}, f32[192,2048]{1,0:T(8,128)S(1)}, u32[]{:S(2)}) %copy-start.1) | copy-done | bytes 1572888
  34.9 2.9 %all-to-all-done.got_in = f32[32,12,128]{2,1,0:T(8,128)} async-done(((f32[32,12,128]{2,1,0:T(8,128)}), f32[32,12,128]{2,1,0:T(8,128)}, u32[]{:S(2)}, u32[]{:S(2)}) %all-to-all-start) | async-done | bytes 196640 | tf_op jit(solution)/shard_map/all_to_all | solution.py:431
  37.9 5.7 %shard_map.105 = f32[192,2048]{1,0:T(8,128)} custom-call(f32[192,2048]{1,0:T(8,128)} %copy-done.1, f32[192,128]{1,0:T(8,128)} %copy-done.2, f32[192,128]{1,0:T(8,128)} %copy-done.3, f32[32,12,128]{2,1,0:T(8,128)} %all-to-all-done.got_in, f32[1,2048]{1,0:T(1,128)} %bitcast.18, s32[6,1,2048]{2,1,0:T(1,128)} %bitcast.14, f32[64,64]{1,0:T(8,128)} %bitcast.22, ...), custom_call_target="tpu_custom_call" | custom-call | tf_op jit(solution)/shard_map/pallas_call | solution.py:358
  (1 shorter events, 0.0 us)
Async XLA Ops:
  0.0 2.4 %copy-start = (f32[1,1,3,64,2048]{4,3,2,1,0:T(8,128)S(1)}, f32[1,1,3,64,2048]{4,3,2,1,0:T(8,128)}, u32[]{:S(2)}) copy-start(f32[1,1,3,64,2048]{4,3,2,1,0:T(8,128)} %param.10) | copy-start | bytes 4718596
  0.0 2.4 %copy-start.10 = (s32[1,1,2,128]{3,2,1,0:T(2,128)S(1)}, s32[1,1,2,128]{3,2,1,0:T(2,128)}, u32[]{:S(2)}) copy-start(s32[1,1,2,128]{3,2,1,0:T(2,128)} %param.14) | copy-start | bytes 3076
  0.0 2.4 %copy-start.8 = (f32[1,1,2048]{2,1,0:T(1,128)S(1)}, f32[1,1,2048]{2,1,0:T(1,128)}, u32[]{:S(2)}) copy-start(f32[1,1,2048]{2,1,0:T(1,128)} %param.11) | copy-start | bytes 24580
  2.4 0.8 %copy-start.4 = (f32[32,4,128]{2,1,0:T(4,128)S(1)}, f32[32,4,128]{2,1,0:T(4,128)}, u32[]{:S(2)}) copy-start(f32[32,4,128]{2,1,0:T(4,128)} %shard_map.100.after) | copy-start | bytes 196612
  3.2 0.9 %copy-start.11 = (bf16[256,384]{1,0:T(8,128)(2,1)S(1)}, bf16[256,384]{1,0:T(8,128)(2,1)}, u32[]{:S(2)}) copy-start(bf16[256,384]{1,0:T(8,128)(2,1)} %constant.2.clone.tables) | copy-start | bytes 589828
  7.2 14.7 %collective-permute-start.3 = (f32[192,128]{1,0:T(8,128)S(1)}, f32[192,128]{1,0:T(8,128)S(1)}, u32[]{:S(2)}, u32[]{:S(2)}) collective-permute-start(f32[192,128]{1,0:T(8,128)S(1)} %get-tuple-element.10), channel_id=1, source_target_pairs={{0,1},{1,2},{2,3},{3,4},{4,5},{5,6},{6,7},{7,8},{8,9},{9,10},{10,1... | collective-permute-start | bytes 294920 | tf_op jit(solution)/shard_map/ppermute | solution.py:423
  9.4 13.8 %copy-start.6 = (s32[1,1,32,2,128]{4,3,2,1,0:T(2,128)S(1)}, s32[1,1,32,2,128]{4,3,2,1,0:T(2,128)}, u32[]{:S(2)}) copy-start(s32[1,1,32,2,128]{4,3,2,1,0:T(2,128)} %param.17) | copy-start | bytes 98308
  9.4 13.8 %copy-start.7 = (f32[1,1,32,128]{3,2,1,0:T(8,128)S(1)}, f32[1,1,32,128]{3,2,1,0:T(8,128)}, u32[]{:S(2)}) copy-start(f32[1,1,32,128]{3,2,1,0:T(8,128)} %param.18) | copy-start | bytes 49156
  9.4 19.9 %copy-start.5 = (s32[1,1,6,2048]{3,1,2,0:T(1,128)S(1)}, s32[1,1,6,2048]{3,1,2,0:T(1,128)}, u32[]{:S(2)}) copy-start(s32[1,1,6,2048]{3,1,2,0:T(1,128)} %param.13) | copy-start | bytes 147460
  9.4 12.5 %collective-permute-start.4 = (f32[192,128]{1,0:T(8,128)S(1)}, f32[192,128]{1,0:T(8,128)S(1)}, u32[]{:S(2)}, u32[]{:S(2)}) collective-permute-start(f32[192,128]{1,0:T(8,128)S(1)} %get-tuple-element.9.after), channel_id=1, source_target_pairs={{1,0},{2,1},{3,2},{4,3},{5,4},{6,5},{7,6},{8,7},{9,8},{10,9},{11,1... | collective-permute-start | bytes 294920 | tf_op jit(solution)/shard_map/ppermute | solution.py:424
  15.7 5.4 %collective-permute-start = (f32[32,4,128]{2,1,0:T(4,128)S(1)}, f32[32,4,128]{2,1,0:T(4,128)S(1)}, u32[]{:S(2)}, u32[]{:S(2)}) collective-permute-start(f32[32,4,128]{2,1,0:T(4,128)S(1)} %copy-done.4), channel_id=1, source_target_pairs={{0,64},{1,65},{2,66},{3,67},{4,68},{5,69},{6,70},{7,71},{8,72},{9,... | collective-permute-start | bytes 196616 | tf_op jit(solution)/shard_map/ppermute | solution.py:408
  18.3 4.9 %collective-permute-start.2 = (f32[32,4,128]{2,1,0:T(4,128)S(1)}, f32[32,4,128]{2,1,0:T(4,128)S(1)}, u32[]{:S(2)}, u32[]{:S(2)}) collective-permute-start(f32[32,4,128]{2,1,0:T(4,128)S(1)} %copy-done.4), channel_id=1, source_target_pairs={{0,32},{1,33},{2,34},{3,35},{4,36},{5,37},{6,38},{7,39},{8,40},{9,... | collective-permute-start | bytes 196616 | tf_op jit(solution)/shard_map/ppermute | solution.py:408
  21.1 2.1 %collective-permute-start.1 = (f32[32,4,128]{2,1,0:T(4,128)S(1)}, f32[32,4,128]{2,1,0:T(4,128)S(1)}, u32[]{:S(2)}, u32[]{:S(2)}) collective-permute-start(f32[32,4,128]{2,1,0:T(4,128)S(1)} %collective-permute-done.got1), channel_id=1, source_target_pairs={{0,32},{1,33},{2,34},{3,35},{4,36},{5,37},{6,38},{7,39},{8,40},{9,... | collective-permute-start | bytes 196616 | tf_op jit(solution)/shard_map/ppermute | solution.py:408
  21.9 0.6 %copy-start.2 = (f32[192,128]{1,0:T(8,128)}, f32[192,128]{1,0:T(8,128)S(1)}, u32[]{:S(2)}) copy-start(f32[192,128]{1,0:T(8,128)S(1)} %collective-permute-done.3.left.left_in) | copy-start | bytes 294916
  21.9 0.7 %copy-start.3 = (f32[192,128]{1,0:T(8,128)}, f32[192,128]{1,0:T(8,128)S(1)}, u32[]{:S(2)}) copy-start(f32[192,128]{1,0:T(8,128)S(1)} %collective-permute-done.4.right.right_in) | copy-start | bytes 294916
  22.6 0.6 %copy-start.9 = (f32[8,128]{1,0:T(8,128)}, f32[8,128]{1,0:T(8,128)S(1)}, u32[]{:S(2)}) copy-start(f32[8,128]{1,0:T(8,128)S(1)} %shard_map.104.after) | copy-start | bytes 12292
  24.7 13.2 %all-to-all-start = ((f32[32,12,128]{2,1,0:T(8,128)}), f32[32,12,128]{2,1,0:T(8,128)}, u32[]{:S(2)}, u32[]{:S(2)}) async-start(f32[32,12,128]{2,1,0:T(8,128)} %shard_map.102.after), calls=%async_computation | async-start | bytes 524288 | tf_op jit(solution)/shard_map/all_to_all | solution.py:431
  33.7 1.2 %copy-start.1 = (f32[192,2048]{1,0:T(8,128)}, f32[192,2048]{1,0:T(8,128)S(1)}, u32[]{:S(2)}) copy-start(f32[192,2048]{1,0:T(8,128)S(1)} %shard_map.103.partial_in) | copy-start | bytes 4718596

commit v3 on v2

--- a/solution.py
+++ b/solution.py
@@ -16,7 +16,7 @@
 BF = jnp.bfloat16
 F32 = jnp.float32
 MIB = 1024 * 1024
-FINAL_LIMIT = 56
+HOLD = 5
 
 
 def gll_matrix():
@@ -33,15 +33,31 @@
 
 
 def derivative_table():
-    matrix = gll_matrix()
-    along_xi = np.kron(np.eye(4), matrix)
-    along_eta = np.kron(matrix, np.eye(4))
-    second = along_xi @ along_xi + along_eta @ along_eta
-    parts = [np.kron(np.eye(8), part).T for part in (along_xi, along_eta, second)]
-    full = np.concatenate(parts, axis=1).astype(np.float32)
-    high = full.astype(BF)
-    low = (full - high.astype(np.float32)).astype(BF)
-    return jnp.asarray(np.concatenate([high, low], axis=0))
+    first = gll_matrix()
+    twice = first @ first
+    m = lax.broadcasted_iota(jnp.int32, (LANES, LANES), 0)
+    n = lax.broadcasted_iota(jnp.int32, (LANES, LANES), 1)
+
+    def entries(a, b, matrices):
+        at = jnp.bitwise_and(a, 3) * 4 + jnp.bitwise_and(b, 3)
+        values = [jnp.zeros((LANES, LANES), F32) for _ in matrices]
+        for row in range(4):
+            for column in range(4):
+                hit = at == column * 4 + row
+                values = [jnp.where(hit, float(p[row, column]), v) for p, v in zip(matrices, values)]
+        return values
+
+    same_row = jnp.right_shift(m, 2) == jnp.right_shift(n, 2)
+    same_element = jnp.right_shift(m, 4) == jnp.right_shift(n, 4)
+    same_column = same_element & (jnp.bitwise_and(m, 3) == jnp.bitwise_and(n, 3))
+    xi, xi_twice = entries(m, n, (first, twice))
+    eta, eta_twice = entries(jnp.right_shift(m, 2), jnp.right_shift(n, 2), (first, twice))
+    parts = [
+        jnp.where(same_row, xi, 0.0),
+        jnp.where(same_column, eta, 0.0),
+        jnp.where(same_row, xi_twice, 0.0) + jnp.where(same_column, eta_twice, 0.0),
+    ]
+    return split(jnp.concatenate(parts, axis=1))
 
 
 def split(values):
@@ -154,7 +170,7 @@
 def atmos_field(values, scale, table_high, table_low):
     third = values.shape[0] // 3
     high, low = split(values)
-    grads = dot(high, table_high) + dot(low, table_high) + dot(high, table_low)
+    grads = dot(jnp.concatenate([high, low], axis=1), table_high) + dot(high, table_low)
     grad_xi = grads[:, :LANES]
     grad_eta = grads[:, LANES : 2 * LANES]
     second = grads[:, 2 * LANES :]
@@ -163,15 +179,18 @@
     return (VISCOSITY * scale * scale) * second - scale * (wind_u * grad_xi + wind_v * grad_eta)
 
 
-def field_kernel(state, metric, tables, rims, after, parts, left_ref, right_ref):
-    atmos = lax.axis_index("comp") != lax.axis_size("comp") - 1
+def fill_parts(atmos, state, metric, parts, tables):
     rows, nodes = state.shape
 
     @pl.when(atmos)
     def _():
+        high, low = derivative_table()
+        tables[:LANES, :] = high
+        tables[LANES : 2 * LANES, :] = high
+        tables[2 * LANES :, :] = low
         for at in range(nodes // LANES):
             where = slice(at * LANES, (at + 1) * LANES)
-            field = atmos_field(state[:, where], metric[0:1, where], tables[:LANES, :], tables[LANES:, :])
+            field = atmos_field(state[:, where], metric[0:1, where], tables[: 2 * LANES, :], tables[2 * LANES :, :])
             high, low = split(field)
             parts[0:rows, where] = high
             parts[rows:, where] = low
@@ -182,25 +201,33 @@
         parts[0:rows, :] = high
         parts[rows:, :] = low
 
+
+def field_kernel(state, metric, rims, left_ref, right_ref, parts, tables):
+    fill_parts(lax.axis_index("comp") != lax.axis_size("comp") - 1, state, metric, parts, tables)
     left_ref[...] = pick_rims(rims[0:1, :], parts)
     right_ref[...] = pick_rims(rims[1:2, :], parts)
 
 
-def inner_kernel(parts, state, metric, links, after, partial, count):
+def inner_kernel(state, metric, links, column, after, partial, rim_count, gains, column_out, count, parts, tables):
     atmos = lax.axis_index("comp") != lax.axis_size("comp") - 1
     rows, nodes = state.shape
     unroll, _, width = count.shape
     chunks = nodes // LANES
+    column_out[...] = column[...]
+    fill_parts(atmos, state, metric, parts, tables)
+
     def run(used, is_ocean):
         def step(at, here):
             where = pl.ds(pl.multiple_of(at * width, width), width)
             index = [links[k, :, where] for k in range(used)]
             number = sum((row >= 0).astype(F32) for row in index)
-            count_links(index, list(range(1, chunks + 1)), here)
-            both = dot(parts[...], here[...])
+            count_links(index, list(range(1, chunks + 1)) + [0, chunks + 1], here)
+            rim_count[0 : here.shape[0] - nodes, where] = here[nodes:, :]
+            both = dot(parts[...], here[0:nodes, :])
             linked = both[:rows] + both[rows:]
             current = state[:, where]
             gain = gain_of(is_ocean, number, metric[0:1, where])
+            gains[0:1, where] = gain
             if is_ocean:
                 partial[:, where] = current + gain * (linked - number * current)
             else:
@@ -223,60 +250,24 @@
         run(6, True)
 
 
-def count_links(index, order, target):
-    width = target.shape[1]
-    one = jnp.ones((16, width), BF)
-    zero = jnp.zeros((16, width), BF)
-    ids = lax.broadcasted_iota(jnp.int16, (16, width), 0)
-    low_off = [
-        jnp.broadcast_to(jnp.bitwise_and(row, LANES - 1), (16, width)).astype(jnp.int16) - ids for row in index
-    ]
-    highs = [jnp.broadcast_to(jnp.right_shift(row, 7), (16, width)).astype(BF) for row in index]
-    masks = [[jnp.where(high == block, one, zero) for high in highs] for block in order]
-    for sub in range(LANES // 16):
-        lows = [jnp.where(off == sub * 16, one, zero) for off in low_off]
-        for slot in range(len(order)):
-            total = None
-            for low, mask in zip(lows, masks[slot]):
-                term = low * mask
-                total = term if total is None else total + term
-            target[slot * LANES + sub * 16 : slot * LANES + sub * 16 + 16, :] = total
-
-def gain_of(ocean, number, metric):
-    return OCEAN_RATE * metric if ocean else ATM_STEP / (1.0 + number)
-
-def rims_there(left, right, token):
-    token[...] = jnp.zeros(token.shape, F32)
-
-
 def final_kernel(
-    partial_in, left_in, right_in, got_in, metric_in, links_in, column_in, after, result,
-    partial, sides, got, metric, links, column, done, rim_parts, count, left_rows, onehots, sems,
+    partial, left, right, got, rim_count, gains, column, result, done, rim_parts, left_rows, onehots, sems
 ):
     comp = lax.axis_index("comp")
     tile = lax.axis_index("tile")
     last_comp = lax.axis_size("comp") - 1
     last_tile = lax.axis_size("tile") - 1
     ocean = comp == last_comp
-    atmos = jnp.logical_not(ocean)
     has_left = jnp.logical_not((tile == 0) & (ocean | (comp == 0)))
     has_right = jnp.logical_not((tile == last_tile) & (comp >= last_comp - 1))
     rows, nodes = partial.shape
     levels = column.shape[0]
     senders = got.shape[0]
-    rim = left_in.shape[1]
-    unroll, _, width = count.shape
+    rim = left.shape[1]
+    width = 2 * LANES
     tiles = nodes // width
     fields = rows // levels
     chunks = nodes // LANES
-    columns = [pl.ds(n * width, width) for n in range(tiles)]
-    moves = [(got_in, got), (links_in, links), (left_in, sides.at[0]), (right_in, sides.at[1])]
-    moves += [(metric_in, metric), (column_in, column)]
-    moves += [(partial_in.at[:, where], partial.at[:, where]) for where in columns]
-    copies = [pltpu.make_async_copy(a, b, sems.at[n]) for n, (a, b) in enumerate(moves)]
-    for copy in copies:
-        copy.start()
-    copies[0].wait()
     ids = lax.broadcasted_iota(jnp.int32, (LANES, LANES), 0)
     ids_high = lax.broadcasted_iota(jnp.int32, (chunks, LANES), 0)
 
@@ -299,10 +290,8 @@
     landed = lax.fori_loop(0, groups, land, jnp.zeros((2 * fields * chunks, LANES), F32))
     forcing = COUPLING * (landed[: fields * chunks] + landed[fields * chunks :])
 
-    for copy in copies[1:6]:
-        copy.wait()
-    for side, there in ((0, has_left), (1, has_right)):
-        high, low = split(jnp.where(there, sides[side], 0.0))
+    for side, there, source in ((0, has_left, left), (1, has_right, right)):
+        high, low = split(jnp.where(there, source[...], 0.0))
         rim_parts[0:rows, side * rim : (side + 1) * rim] = high
         rim_parts[rows:, side * rim : (side + 1) * rim] = low
     col_high, col_low = split(column[...])
@@ -310,42 +299,28 @@
     col = jnp.concatenate([col_high, col_low], axis=0)
 
     def move(at):
-        return pltpu.make_async_copy(done.at[:, columns[at]], result.at[:, columns[at]], sems.at[6 + tiles + at])
-
-    def run(used, is_ocean):
-        for at in range(tiles):
-            where = slice(at * width, (at + 1) * width)
-            here = count.at[at % unroll]
-            index = [links[k, :, where] for k in range(used)]
-            number = sum((row >= 0).astype(F32) for row in index)
-            count_links(index, [0, chunks + 1], here)
-            both = dot(rim_parts[...], here[...])
-            gain = gain_of(is_ocean, number, metric[0:1, where])
-            copies[6 + at].wait()
-            updated = partial[:, where] + gain * (both[:rows] + both[rows:])
-            uh, ul = split(updated)
-            for f in range(fields):
-                part = slice(f * levels, (f + 1) * levels)
-                full = dot(col, uh[part])
-                mixed = full[:levels] + full[levels:] + dot(col_high, ul[part])
-                first = f * chunks + at * width // LANES
-                rows_of = [forcing[n : n + 1, :] for n in range(first, first + width // LANES)]
-                done[part, where] = mixed + col_gain * jnp.concatenate(rows_of, axis=1)
-            move(at).start()
-
-    @pl.when(atmos)
-    def _():
-        run(3, False)
-
-    @pl.when(ocean)
-    def _():
-        run(6, True)
+        where = pl.ds(at * width, width)
+        return pltpu.make_async_copy(done.at[:, where], result.at[:, where], sems.at[at])
+
+    for at in range(tiles):
+        where = slice(at * width, (at + 1) * width)
+        both = dot(rim_parts[...], rim_count[0 : 2 * rim, where])
+        updated = partial[:, where] + gains[0:1, where] * (both[:rows] + both[rows:])
+        uh, ul = split(updated)
+        for f in range(fields):
+            part = slice(f * levels, (f + 1) * levels)
+            full = dot(col, uh[part])
+            mixed = full[:levels] + full[levels:] + dot(col_high, ul[part])
+            first = f * chunks + at * width // LANES
+            rows_of = [forcing[n : n + 1, :] for n in range(first, first + width // LANES)]
+            done[part, where] = mixed + col_gain * jnp.concatenate(rows_of, axis=1)
+        move(at).start()
 
     for at in range(tiles):
         move(at).wait()
 
 
-def call(kernel, args, outs, scratch=(), limit=32, form="vmem", anywhere=(), cost=None):
+def call(kernel, args, outs, scratch=(), limit=32, form="vmem", anywhere=(), out_far=(), cost=None):
     free = pl.BlockSpec(memory_space=pl.ANY)
     whole = pl.BlockSpec(memory_space=pltpu.VMEM)
 
@@ -359,7 +334,7 @@
         kernel,
         grid=(1,) if form == "block" else (),
         in_specs=[free if n in anywhere else spec(arg.shape) for n, arg in enumerate(args)],
-        out_specs=[spec(out.shape) for out in outs],
+        out_specs=[free if n in out_far else spec(out.shape) for n, out in enumerate(outs)],
         out_shape=outs,
         scratch_shapes=list(scratch),
         compiler_params=params,
@@ -381,7 +356,6 @@
     tiles = nodes // width
     metric_row = metric.reshape(1, nodes)
     link_rows = links.reshape(6, 1, nodes)
-    tables = derivative_table()
     dma = pltpu.SemaphoreType.DMA
     int32 = jnp.int32
 
@@ -407,16 +381,17 @@
         pairs = [(a * ntile + b, (a ^ flip) * ntile + b) for a in range(ncomp) for b in range(ntile)]
         return lax.ppermute(values, axes, pairs)
 
+    got0 = across(payload, 3)
     got1 = across(payload, 2)
     got2 = across(payload, 1)
-    got0 = across(got1, 1)
 
     current = state.reshape(rows, nodes)
-    parts, to_left, to_right = call(
+    to_left, to_right = call(
         field_kernel,
-        (current, metric_row, tables, rims.reshape(2, rim), payload),
-        [shape(2 * rows, nodes, kind=BF), shape(rows, rim), shape(rows, rim)],
-        anywhere=(4,),
+        (current, metric_row, rims.reshape(2, rim)),
+        [shape(rows, rim), shape(rows, rim)],
+        [held(2 * rows, nodes, kind=BF), held(3 * LANES, 3 * LANES, kind=BF)],
+
         cost=4_000_000_000,
     )
     steps = [(i, (i + 1) % total) for i in range(total)]
@@ -430,36 +405,26 @@
     )
     got = lax.all_to_all(rows_out, "tile", split_axis=0, concat_axis=0, tiled=True)
 
-    (partial,) = call(
+    partial, rim_count, gains, column = call(
         inner_kernel,
-        (parts, current, metric_row, link_rows, rows_out),
-        [shape(rows, nodes)],
-        [held(2, nodes, width, kind=BF)],
+        (current, metric_row, link_rows, column_op.reshape(levels, levels), rows_out),
+        [shape(rows, nodes), shape(HOLD * rim, nodes, kind=BF), shape(1, nodes), shape(levels, levels)],
+        [held(2, nodes + 2 * rim, width, kind=BF), held(2 * rows, nodes, kind=BF), held(3 * LANES, 3 * LANES, kind=BF)],
         anywhere=(4,),
         cost=8_000_000_000,
     )
-
-    (rims_token,) = call(rims_there, (left, right), [shape(8, LANES)], anywhere=(0, 1), cost=8_000_000_000)
     (result,) = call(
         final_kernel,
-        (partial, left, right, got, metric_row, link_rows, column_op.reshape(levels, levels), rims_token),
+        (partial, left, right, got, rim_count, gains, column),
         [shape(rows, nodes)],
         [
             held(rows, nodes),
-            held(2, rows, rim),
-            held(ntile, (ncomp - 1) * (fields + 1), slot),
-            held(1, nodes),
-            held(6, 1, nodes, kind=int32),
-            held(levels, levels),
-            held(rows, nodes),
             held(2 * rows, 2 * rim, kind=BF),
-            held(2, 2 * rim, width, kind=BF),
             held(2 * fields * chunks, ntile * slot, kind=BF),
             held(LANES, ntile * slot, kind=BF),
-            dma((6 + 2 * tiles,)),
+            dma((tiles,)),
         ],
-        limit=FINAL_LIMIT,
-        form="any",
+        out_far=(0,),
     )
     return result.reshape(state.shape)
 

time: 43.9 us -> 37.8 us (0.86)
  waiting for transfers between devices: 5.75 us -> 0.02 us
    all_to_all x1, waiting for transfers between devices: 2.95 us -> 0.01 us  [per_device(): lax.all_to_all(rows_out, 'tile', split_axis=0, concat_axis=0, tiled=True)]
    ppermute x3, waiting for transfers between devices: 2.8 us -> 0.01 us  [across(): return lax.ppermute(values, axes, pairs)]
    ppermute x3, starting transfers between devices: 3.4 us -> 4.56 us  [across(): return lax.ppermute(values, axes, pairs)]
    ppermute x1, starting transfers between devices: 2.2 us -> 1.45 us  [per_device(): left = lax.ppermute(to_right, axes, steps)]
    ppermute x1, starting transfers between devices: 6.34 us -> 5.86 us  [per_device(): right = lax.ppermute(to_left, axes, [(b, a) for a, b in steps])]
    pallas_call x5 -> x4, Pallas kernels: 14.5 us -> 14.9 us  [call(): pl.pallas_call(kernel, grid=(1,) if form == 'block' else (), in_specs=[fr...]
    unnamed x24 -> x20, local copies, waits for them, and re-layouts: 4.21 us -> 3.98 us
  transfers between devices with their start and end apart: 6 -> 6, of which waited for: 2 -> 0; matrix products, arithmetic and copies ran while one was open for 0% -> 0% of each run, Pallas kernels for 10% -> 29%
where the time goes in v3:
time: 37.8 us; the launch traced here: 37.5 us
  Pallas kernels  17.3 us (46%)
  starting transfers between devices  16.2 us (43%)
  local copies, waits for them, and re-layouts  3.98 us (11%)
    pallas_call x4, Pallas kernels, call(): pl.pallas_call(kernel, grid=(1,) if form == 'block' else (), in_specs=[fr...  14.9 us
    ppermute x1, starting transfers between devices, per_device(): right = lax.ppermute(to_left, axes, [(b, a) for a, b in steps])  5.86 us
    ppermute x3, starting transfers between devices, across(): return lax.ppermute(values, axes, pairs)  4.56 us
    all_to_all x1, starting transfers between devices, per_device(): lax.all_to_all(rows_out, 'tile', split_axis=0, concat_axis=0, tiled=True)  4.28 us
    unnamed x20, local copies, waits for them, and re-layouts  3.98 us
    pallas_call x1, Pallas kernels, per_device(): pl.pallas_call(out_kernel, grid=(1,), in_specs=[pl.BlockSpec((fields, 8,...  2.36 us
    ppermute x1, starting transfers between devices, per_device(): left = lax.ppermute(to_right, axes, steps)  1.45 us
  transfers between devices with their start and end apart: 6, of which 0 were waited for; matrix products, arithmetic and copies ran while one was open for 0% of the time, Pallas kernels for 29%

profile of v3, /device:TPU:1, one launch (start us, length us, event | category | flops | bytes accessed | tf_op | source)
XLA Modules:
  0.0 37.5 jit_solution(2205814272365347412)
XLA Ops:
  0.0 0.0 copy-start
  0.0 0.0 copy-start.9
  0.0 0.0 copy-start.8
  0.0 2.4 %shard_map.91 = f32[32,4,128]{2,1,0:T(4,128)} custom-call(f32[3,64,2048]{2,1,0:T(8,128)} %bitcast.11, s32[32,2,128]{2,1,0:T(2,128)} %bitcast.21, f32[32,128]{1,0:T(8,128)} %bitcast.22), custom_call_target="tpu_custom_call" | custom-call | tf_op jit(solution)/shard_map/pallas_call | solution.py:368
  2.4 1.4 %collective-permute-start.2 = (f32[32,4,128]{2,1,0:T(4,128)}, f32[32,4,128]{2,1,0:T(4,128)S(1)}, u32[]{:S(2)}, u32[]{:S(2)}) collective-permute-start(f32[32,4,128]{2,1,0:T(4,128)} %shard_map.91), channel_id=1, source_target_pairs={{0,32},{1,33},{2,34},{3,35},{4,36},{5,37},{6,38},{7,39},{8,40},{9,... | collective-permute-start | bytes 196616 | tf_op jit(solution)/shard_map/ppermute | solution.py:382
  3.8 3.0 %collective-permute-start.1 = (f32[32,4,128]{2,1,0:T(4,128)}, f32[32,4,128]{2,1,0:T(4,128)S(1)}, u32[]{:S(2)}, u32[]{:S(2)}) collective-permute-start(f32[32,4,128]{2,1,0:T(4,128)} %shard_map.91), channel_id=1, source_target_pairs={{0,64},{1,65},{2,66},{3,67},{4,68},{5,69},{6,70},{7,71},{8,72},{9,... | collective-permute-start | bytes 196616 | tf_op jit(solution)/shard_map/ppermute | solution.py:382
  6.8 0.1 collective-permute-start
  6.9 0.0 copy-done
  6.9 0.0 copy-done.9
  6.9 0.0 copy-done.8
  6.9 0.0 copy-start.4
  6.9 0.0 copy-start.5
  7.0 0.0 copy-start.6
  7.0 0.0 copy-start.7
  7.0 2.9 %shard_map.92 = (f32[192,128]{1,0:T(8,128)S(1)}, f32[192,128]{1,0:T(8,128)S(1)}) custom-call(f32[192,2048]{1,0:T(8,128)S(1)} %bitcast.12, f32[1,2048]{1,0:T(1,128)S(1)} %bitcast.18, s32[2,128]{1,0:T(2,128)S(1)} %bitcast.20), custom_call_target="tpu_custom_call" | custom-call | flops 4000000000 | bytes 4000000 | tf_op jit(solution)/shard_map/pallas_call | solution.py:333
  9.9 1.5 %collective-permute-start.3 = (f32[192,128]{1,0:T(8,128)S(1)}, f32[192,128]{1,0:T(8,128)S(1)}, u32[]{:S(2)}, u32[]{:S(2)}) collective-permute-start(f32[192,128]{1,0:T(8,128)S(1)} %get-tuple-element.13), channel_id=1, source_target_pairs={{0,1},{1,2},{2,3},{3,4},{4,5},{5,6},{6,7},{7,8},{8,9},{9,10},{10,1... | collective-permute-start | bytes 294920 | tf_op jit(solution)/shard_map/ppermute | solution.py:398
  11.4 5.9 %collective-permute-start.4 = (f32[192,128]{1,0:T(8,128)S(1)}, f32[192,128]{1,0:T(8,128)S(1)}, u32[]{:S(2)}, u32[]{:S(2)}) collective-permute-start(f32[192,128]{1,0:T(8,128)S(1)} %get-tuple-element.11.after), channel_id=1, source_target_pairs={{1,0},{2,1},{3,2},{4,3},{5,4},{6,5},{7,6},{8,7},{9,8},{10,9},{11,1... | collective-permute-start | bytes 294920 | tf_op jit(solution)/shard_map/ppermute | solution.py:399
  17.2 0.0 collective-permute-done.2.got2
  17.2 0.0 collective-permute-done.1.got1
  17.2 0.0 collective-permute-done.got0
  17.2 0.0 copy-done.4
  17.2 0.0 copy-done.5
  17.2 1.4 %shard_map.93.after = f32[32,12,128]{2,1,0:T(8,128)} custom-call(f32[32,4,128]{2,1,0:T(4,128)S(1)} %collective-permute-done.got0, f32[32,4,128]{2,1,0:T(4,128)S(1)} %collective-permute-done.1.got1, f32[32,4,128]{2,1,0:T(4,128)S(1)} %collective-permute-done.2.got2, s32[32,2,128]{2,1,0:T(2,128)S(1)} %bitcast.14, f32[32,128]{1,0:T(8,128)S(1)} %bitcast.15, ...), custom_call_target="tpu_custom_call" | custom-call | tf_op jit(solution)/shard_map/pallas_call | solution.py:333
  18.7 4.3 %all-to-all-start = ((f32[32,12,128]{2,1,0:T(8,128)}), f32[32,12,128]{2,1,0:T(8,128)S(1)}, u32[]{:S(2)}, u32[]{:S(2)}) async-start(f32[32,12,128]{2,1,0:T(8,128)} %shard_map.93.after), calls=%async_computation | async-start | bytes 524288 | tf_op jit(solution)/shard_map/all_to_all | solution.py:406
  23.0 0.0 copy-done.6
  23.0 0.0 copy-done.7
  23.0 0.0 copy-start.1
  23.0 1.4 %copy-done.1 = f32[1,1,3,64,2048]{4,3,2,1,0:T(8,128)S(1)} copy-done((f32[1,1,3,64,2048]{4,3,2,1,0:T(8,128)S(1)}, f32[1,1,3,64,2048]{4,3,2,1,0:T(8,128)}, u32[]{:S(2)}) %copy-start.1) | copy-done | bytes 1572888
  24.4 6.5 %shard_map.94 = (f32[192,2048]{1,0:T(8,128)S(1)}, bf16[640,2048]{1,0:T(8,128)(2,1)S(1)}, f32[1,2048]{1,0:T(1,128)S(1)}, f32[64,64]{1,0:T(8,128)S(1)}) custom-call(f32[192,2048]{1,0:T(8,128)S(1)} %bitcast.13, f32[1,2048]{1,0:T(1,128)S(1)} %bitcast.19, s32[6,1,2048]{2,1,0:T(1,128)S(1)} %bitcast.16, f32[64,64]{1,0:T(8,128)S(1)} %bitcast.17, ...), custom_call_target="tpu_custom_call" | custom-call | flops 8000000000 | bytes 4000000 | tf_op jit(solution)/shard_map/pallas_call | solution.py:333
  30.9 0.0 copy-start.2
  30.9 1.1 %copy-done.2 = f32[192,2048]{1,0:T(8,128)} copy-done((f32[192,2048]{1,0:T(8,128)}, f32[192,2048]{1,0:T(8,128)S(1)}, u32[]{:S(2)}) %copy-start.2) | copy-done | bytes 1572888
  32.1 0.0 collective-permute-done.3.left
  32.1 0.0 collective-permute-done.4.right
  32.1 0.0 all-to-all-done.got
  32.1 0.0 copy-start.3
  32.1 1.4 %copy-done.3 = f32[192,2048]{1,0:T(8,128)S(1)} copy-done((f32[192,2048]{1,0:T(8,128)S(1)}, f32[192,2048]{1,0:T(8,128)}, u32[]{:S(2)}) %copy-start.3) | copy-done | bytes 1572888
  33.5 4.1 %shard_map.95 = f32[192,2048]{1,0:T(8,128)} custom-call(f32[192,2048]{1,0:T(8,128)S(1)} %copy-done.3, f32[192,128]{1,0:T(8,128)S(1)} %collective-permute-done.3.left, f32[192,128]{1,0:T(8,128)S(1)} %collective-permute-done.4.right, f32[32,12,128]{2,1,0:T(8,128)S(1)} %all-to-all-done.got, bf16[640,2048]{1,0:T(8,128)(2,1)S(1)} %get-tuple-element.14.rim_count, ...), custom_call_target="tpu_custom_call" | custom-call | tf_op jit(solution)/shard_map/pallas_call | solution.py:333
Async XLA Ops:
  0.0 6.9 %copy-start = (f32[1,1,3,64,2048]{4,3,2,1,0:T(8,128)S(1)}, f32[1,1,3,64,2048]{4,3,2,1,0:T(8,128)}, u32[]{:S(2)}) copy-start(f32[1,1,3,64,2048]{4,3,2,1,0:T(8,128)} %param.9) | copy-start | bytes 4718596
  0.0 6.9 %copy-start.9 = (s32[1,1,2,128]{3,2,1,0:T(2,128)S(1)}, s32[1,1,2,128]{3,2,1,0:T(2,128)}, u32[]{:S(2)}) copy-start(s32[1,1,2,128]{3,2,1,0:T(2,128)} %param.13) | copy-start | bytes 3076
  0.0 6.9 %copy-start.8 = (f32[1,1,2048]{2,1,0:T(1,128)S(1)}, f32[1,1,2048]{2,1,0:T(1,128)}, u32[]{:S(2)}) copy-start(f32[1,1,2048]{2,1,0:T(1,128)} %param.10) | copy-start | bytes 24580
  2.4 14.9 %collective-permute-start.2 = (f32[32,4,128]{2,1,0:T(4,128)}, f32[32,4,128]{2,1,0:T(4,128)S(1)}, u32[]{:S(2)}, u32[]{:S(2)}) collective-permute-start(f32[32,4,128]{2,1,0:T(4,128)} %shard_map.91), channel_id=1, source_target_pairs={{0,32},{1,33},{2,34},{3,35},{4,36},{5,37},{6,38},{7,39},{8,40},{9,... | collective-permute-start | bytes 196616 | tf_op jit(solution)/shard_map/ppermute | solution.py:382
  3.8 13.4 %collective-permute-start.1 = (f32[32,4,128]{2,1,0:T(4,128)}, f32[32,4,128]{2,1,0:T(4,128)S(1)}, u32[]{:S(2)}, u32[]{:S(2)}) collective-permute-start(f32[32,4,128]{2,1,0:T(4,128)} %shard_map.91), channel_id=1, source_target_pairs={{0,64},{1,65},{2,66},{3,67},{4,68},{5,69},{6,70},{7,71},{8,72},{9,... | collective-permute-start | bytes 196616 | tf_op jit(solution)/shard_map/ppermute | solution.py:382
  6.8 10.4 %collective-permute-start = (f32[32,4,128]{2,1,0:T(4,128)}, f32[32,4,128]{2,1,0:T(4,128)S(1)}, u32[]{:S(2)}, u32[]{:S(2)}) collective-permute-start(f32[32,4,128]{2,1,0:T(4,128)} %shard_map.91), channel_id=1, source_target_pairs={{0,96},{1,97},{2,98},{3,99},{4,100},{5,101},{6,102},{7,103},{8,104... | collective-permute-start | bytes 196616 | tf_op jit(solution)/shard_map/ppermute | solution.py:382
  6.9 10.3 %copy-start.4 = (s32[1,1,32,2,128]{4,3,2,1,0:T(2,128)S(1)}, s32[1,1,32,2,128]{4,3,2,1,0:T(2,128)}, u32[]{:S(2)}) copy-start(s32[1,1,32,2,128]{4,3,2,1,0:T(2,128)} %param.16) | copy-start | bytes 98308
  6.9 10.3 %copy-start.5 = (f32[1,1,32,128]{3,2,1,0:T(8,128)S(1)}, f32[1,1,32,128]{3,2,1,0:T(8,128)}, u32[]{:S(2)}) copy-start(f32[1,1,32,128]{3,2,1,0:T(8,128)} %param.17) | copy-start | bytes 49156
  7.0 16.0 %copy-start.6 = (s32[1,1,6,2048]{3,1,2,0:T(1,128)S(1)}, s32[1,1,6,2048]{3,1,2,0:T(1,128)}, u32[]{:S(2)}) copy-start(s32[1,1,6,2048]{3,1,2,0:T(1,128)} %param.12) | copy-start | bytes 147460
  7.0 16.0 %copy-start.7 = (f32[1,64,64]{2,1,0:T(8,128)S(1)}, f32[1,64,64]{2,1,0:T(8,128)}, u32[]{:S(2)}) copy-start(f32[1,64,64]{2,1,0:T(8,128)} %param.11) | copy-start | bytes 49156
  9.9 22.2 %collective-permute-start.3 = (f32[192,128]{1,0:T(8,128)S(1)}, f32[192,128]{1,0:T(8,128)S(1)}, u32[]{:S(2)}, u32[]{:S(2)}) collective-permute-start(f32[192,128]{1,0:T(8,128)S(1)} %get-tuple-element.13), channel_id=1, source_target_pairs={{0,1},{1,2},{2,3},{3,4},{4,5},{5,6},{6,7},{7,8},{8,9},{9,10},{10,1... | collective-permute-start | bytes 294920 | tf_op jit(solution)/shard_map/ppermute | solution.py:398
  11.4 20.7 %collective-permute-start.4 = (f32[192,128]{1,0:T(8,128)S(1)}, f32[192,128]{1,0:T(8,128)S(1)}, u32[]{:S(2)}, u32[]{:S(2)}) collective-permute-start(f32[192,128]{1,0:T(8,128)S(1)} %get-tuple-element.11.after), channel_id=1, source_target_pairs={{1,0},{2,1},{3,2},{4,3},{5,4},{6,5},{7,6},{8,7},{9,8},{10,9},{11,1... | collective-permute-start | bytes 294920 | tf_op jit(solution)/shard_map/ppermute | solution.py:399
  18.7 13.4 %all-to-all-start = ((f32[32,12,128]{2,1,0:T(8,128)}), f32[32,12,128]{2,1,0:T(8,128)S(1)}, u32[]{:S(2)}, u32[]{:S(2)}) async-start(f32[32,12,128]{2,1,0:T(8,128)} %shard_map.93.after), calls=%async_computation | async-start | bytes 524288 | tf_op jit(solution)/shard_map/all_to_all | solution.py:406
  23.0 1.4 %copy-start.1 = (f32[1,1,3,64,2048]{4,3,2,1,0:T(8,128)S(1)}, f32[1,1,3,64,2048]{4,3,2,1,0:T(8,128)}, u32[]{:S(2)}) copy-start(f32[1,1,3,64,2048]{4,3,2,1,0:T(8,128)} %param.9) | copy-start | bytes 4718596
  30.9 1.1 %copy-start.2 = (f32[192,2048]{1,0:T(8,128)}, f32[192,2048]{1,0:T(8,128)S(1)}, u32[]{:S(2)}) copy-start(f32[192,2048]{1,0:T(8,128)S(1)} %get-tuple-element.12.partial) | copy-start | bytes 4718596
  32.1 1.4 %copy-start.3 = (f32[192,2048]{1,0:T(8,128)S(1)}, f32[192,2048]{1,0:T(8,128)}, u32[]{:S(2)}) copy-start(f32[192,2048]{1,0:T(8,128)} %copy-done.2) | copy-start | bytes 4718596

commit v4 on v3

--- a/solution.py
+++ b/solution.py
@@ -16,7 +16,6 @@
 BF = jnp.bfloat16
 F32 = jnp.float32
 MIB = 1024 * 1024
-HOLD = 5
 
 
 def gll_matrix():
@@ -202,18 +201,20 @@
         parts[rows:, :] = low
 
 
-def field_kernel(state, metric, rims, left_ref, right_ref, parts, tables):
+def field_kernel(state, metric, rims, state_here, left_ref, right_ref, parts, tables):
+    state_here[...] = state[...]
     fill_parts(lax.axis_index("comp") != lax.axis_size("comp") - 1, state, metric, parts, tables)
     left_ref[...] = pick_rims(rims[0:1, :], parts)
     right_ref[...] = pick_rims(rims[1:2, :], parts)
 
 
-def inner_kernel(state, metric, links, column, after, partial, rim_count, gains, column_out, count, parts, tables):
+def inner_kernel(state, metric, links, column, after, partial, gains, links_out, column_out, count, parts, tables):
     atmos = lax.axis_index("comp") != lax.axis_size("comp") - 1
     rows, nodes = state.shape
     unroll, _, width = count.shape
     chunks = nodes // LANES
     column_out[...] = column[...]
+    links_out[...] = links[...]
     fill_parts(atmos, state, metric, parts, tables)
 
     def run(used, is_ocean):
@@ -221,9 +222,8 @@
             where = pl.ds(pl.multiple_of(at * width, width), width)
             index = [links[k, :, where] for k in range(used)]
             number = sum((row >= 0).astype(F32) for row in index)
-            count_links(index, list(range(1, chunks + 1)) + [0, chunks + 1], here)
-            rim_count[0 : here.shape[0] - nodes, where] = here[nodes:, :]
-            both = dot(parts[...], here[0:nodes, :])
+            count_links(index, list(range(1, chunks + 1)), here)
+            both = dot(parts[...], here[...])
             linked = both[:rows] + both[rows:]
             current = state[:, where]
             gain = gain_of(is_ocean, number, metric[0:1, where])
@@ -251,7 +251,7 @@
 
 
 def final_kernel(
-    partial, left, right, got, rim_count, gains, column, result, done, rim_parts, left_rows, onehots, sems
+    partial, left, right, got, gains, links, column, result, done, rim_parts, left_rows, onehots, count, wide, sems
 ):
     comp = lax.axis_index("comp")
     tile = lax.axis_index("tile")
@@ -268,22 +268,27 @@
     tiles = nodes // width
     fields = rows // levels
     chunks = nodes // LANES
-    ids = lax.broadcasted_iota(jnp.int32, (LANES, LANES), 0)
-    ids_high = lax.broadcasted_iota(jnp.int32, (chunks, LANES), 0)
+    ids = lax.broadcasted_iota(jnp.int16, (LANES, LANES), 0)
+    ids_high = lax.broadcasted_iota(jnp.int16, (chunks, LANES), 0)
+    one = jnp.ones((), BF)
+    zero = jnp.zeros((), BF)
 
     def land(part, total):
         for a in range(senders):
-            base = 4 * part
-            cell = got[a, pl.ds(base + fields, 1), :].astype(jnp.int32)
-            lane_low = jnp.bitwise_and(cell, LANES - 1)
-            lane_high = jnp.right_shift(cell, 7)
+            base_row = 4 * part
+            cell = got[a, pl.ds(base_row + fields, 1), :].astype(jnp.int32)
+            lane_low = jnp.broadcast_to(jnp.bitwise_and(cell, LANES - 1), (chunks, LANES)).astype(jnp.int16)
+            lane_high = jnp.broadcast_to(jnp.right_shift(cell, 7), (chunks, LANES)).astype(jnp.int16)
+            wanted = jnp.broadcast_to(lane_low[None], (LANES // chunks, chunks, LANES)).reshape(LANES, LANES)
             where = slice(a * LANES, (a + 1) * LANES)
-            onehots[:, where] = jnp.where(ids == lane_low, 1.0, 0.0).astype(BF)
+            onehots[:, where] = jnp.where(ids == wanted, one, zero)
             mask = ids_high == lane_high
-            picked = [jnp.where(mask, got[a, pl.ds(base + f, 1), :], 0.0) for f in range(fields)]
-            high, low = split(jnp.concatenate(picked, axis=0))
-            left_rows[0 : fields * chunks, where] = high
-            left_rows[fields * chunks :, where] = low
+            for f in range(fields):
+                row = got[a, pl.ds(base_row + f, 1), :]
+                high = row.astype(BF).astype(F32)
+                for n, value in ((f, high), (fields + f, row - high)):
+                    spread = jnp.broadcast_to(value, (chunks, LANES)).astype(BF)
+                    left_rows[n * chunks : (n + 1) * chunks, where] = jnp.where(mask, spread, zero)
         return total + dot_nt(left_rows[...], onehots[...])
 
     groups = jnp.where(ocean, last_comp, 1)
@@ -294,33 +299,48 @@
         high, low = split(jnp.where(there, source[...], 0.0))
         rim_parts[0:rows, side * rim : (side + 1) * rim] = high
         rim_parts[rows:, side * rim : (side + 1) * rim] = low
-    col_high, col_low = split(column[...])
+    wide[...] = jnp.zeros(wide.shape, F32)
+    for f in range(fields):
+        at = f * levels
+        wide[at : at + levels, at : at + levels] = column[...]
+    col_high, col_low = split(wide[:, 0:rows])
+    col = jnp.concatenate([col_high, col_low], axis=0)
     col_gain = column[:, 0:1]
-    col = jnp.concatenate([col_high, col_low], axis=0)
 
     def move(at):
         where = pl.ds(at * width, width)
         return pltpu.make_async_copy(done.at[:, where], result.at[:, where], sems.at[at])
 
-    for at in range(tiles):
-        where = slice(at * width, (at + 1) * width)
-        both = dot(rim_parts[...], rim_count[0 : 2 * rim, where])
-        updated = partial[:, where] + gains[0:1, where] * (both[:rows] + both[rows:])
-        uh, ul = split(updated)
-        for f in range(fields):
-            part = slice(f * levels, (f + 1) * levels)
-            full = dot(col, uh[part])
-            mixed = full[:levels] + full[levels:] + dot(col_high, ul[part])
-            first = f * chunks + at * width // LANES
-            rows_of = [forcing[n : n + 1, :] for n in range(first, first + width // LANES)]
-            done[part, where] = mixed + col_gain * jnp.concatenate(rows_of, axis=1)
-        move(at).start()
+    def run(used):
+        for at in range(tiles):
+            where = slice(at * width, (at + 1) * width)
+            here = count.at[at % 2]
+            count_links([links[k, :, where] for k in range(used)], [0, chunks + 1], here)
+            both = dot(rim_parts[...], here[...])
+            updated = partial[:, where] + gains[0:1, where] * (both[:rows] + both[rows:])
+            high, low = split(updated)
+            full = dot(col, high)
+            mixed = full[:rows] + full[rows:] + dot(col_high, low)
+            for f in range(fields):
+                part = slice(f * levels, (f + 1) * levels)
+                first = f * chunks + at * width // LANES
+                rows_of = [forcing[n : n + 1, :] for n in range(first, first + width // LANES)]
+                done[part, where] = mixed[part] + col_gain * jnp.concatenate(rows_of, axis=1)
+            move(at).start()
+
+    @pl.when(jnp.logical_not(ocean))
+    def _():
+        run(3)
+
+    @pl.when(ocean)
+    def _():
+        run(6)
 
     for at in range(tiles):
         move(at).wait()
 
 
-def call(kernel, args, outs, scratch=(), limit=32, form="vmem", anywhere=(), out_far=(), cost=None):
+def call(kernel, args, outs, scratch=(), limit=32, form="vmem", anywhere=(), out_far=(), cost=None, alias=None):
     free = pl.BlockSpec(memory_space=pl.ANY)
     whole = pl.BlockSpec(memory_space=pltpu.VMEM)
 
@@ -338,6 +358,7 @@
         out_shape=outs,
         scratch_shapes=list(scratch),
         compiler_params=params,
+        input_output_aliases=alias or {},
         cost_estimate=cost and pl.CostEstimate(flops=cost, bytes_accessed=4_000_000, transcendentals=0),
     )(*args)
 
@@ -386,10 +407,10 @@
     got2 = across(payload, 1)
 
     current = state.reshape(rows, nodes)
-    to_left, to_right = call(
+    state_here, to_left, to_right = call(
         field_kernel,
         (current, metric_row, rims.reshape(2, rim)),
-        [shape(rows, rim), shape(rows, rim)],
+        [shape(rows, nodes), shape(rows, rim), shape(rows, rim)],
         [held(2 * rows, nodes, kind=BF), held(3 * LANES, 3 * LANES, kind=BF)],
 
         cost=4_000_000_000,
@@ -399,29 +420,32 @@
     right = lax.ppermute(to_left, axes, [(b, a) for a, b in steps])
     (rows_out,) = call(
         back_kernel,
-        (got0, got1, got2, back_map.reshape(ntile, 2, slot), back_weight.reshape(ntile, slot), to_left),
+        (got0, got1, got2, back_map.reshape(ntile, 2, slot), back_weight.reshape(ntile, slot), to_right),
         [shape(ntile, (ncomp - 1) * (fields + 1), slot)],
         anywhere=(5,),
     )
     got = lax.all_to_all(rows_out, "tile", split_axis=0, concat_axis=0, tiled=True)
 
-    partial, rim_count, gains, column = call(
+    partial, gains, links_here, column = call(
         inner_kernel,
-        (current, metric_row, link_rows, column_op.reshape(levels, levels), rows_out),
-        [shape(rows, nodes), shape(HOLD * rim, nodes, kind=BF), shape(1, nodes), shape(levels, levels)],
-        [held(2, nodes + 2 * rim, width, kind=BF), held(2 * rows, nodes, kind=BF), held(3 * LANES, 3 * LANES, kind=BF)],
+        (state_here, metric_row, link_rows, column_op.reshape(levels, levels), rows_out),
+        [shape(rows, nodes), shape(1, nodes), shape(6, 1, nodes, kind=int32), shape(levels, levels)],
+        [held(2, nodes, width, kind=BF), held(2 * rows, nodes, kind=BF), held(3 * LANES, 3 * LANES, kind=BF)],
         anywhere=(4,),
         cost=8_000_000_000,
+        alias={0: 0},
     )
     (result,) = call(
         final_kernel,
-        (partial, left, right, got, rim_count, gains, column),
+        (partial, left, right, got, gains, links_here, column),
         [shape(rows, nodes)],
         [
             held(rows, nodes),
             held(2 * rows, 2 * rim, kind=BF),
             held(2 * fields * chunks, ntile * slot, kind=BF),
             held(LANES, ntile * slot, kind=BF),
+            held(2, 2 * rim, width, kind=BF),
+            held(rows, width),
             dma((tiles,)),
         ],
         out_far=(0,),

time: 37.8 us -> 35.5 us (0.939)
  local copies, waits for them, and re-layouts: 3.98 us -> 0.03 us
  waiting for transfers between devices: 0.02 us -> 2.51 us
  Pallas kernels: 17.3 us -> 16.8 us
  starting transfers between devices: 16.2 us -> 15.7 us
    unnamed x20 -> x14, local copies, waits for them, and re-layouts: 3.98 us -> 0.03 us
    all_to_all x1, waiting for transfers between devices: 0.01 us -> 2.5 us  [per_device(): lax.all_to_all(rows_out, 'tile', split_axis=0, concat_axis=0, tiled=True)]
    pallas_call x4, Pallas kernels: 14.9 us -> 14.4 us  [call(): pl.pallas_call(kernel, grid=(1,) if form == 'block' else (), in_specs=[fr...]
    all_to_all x1, starting transfers between devices: 4.28 us -> 3.87 us  [per_device(): lax.all_to_all(rows_out, 'tile', split_axis=0, concat_axis=0, tiled=True)]
  transfers between devices with their start and end apart: 6 -> 6, of which waited for: 0 -> 1; matrix products, arithmetic and copies ran while one was open for 0% -> 0% of each run, Pallas kernels for 29% -> 30%
where the time goes in v4:
time: 35.5 us; the launch traced here: 35.3 us
  Pallas kernels  16.8 us (47%)
  starting transfers between devices  15.7 us (44%)
  waiting for transfers between devices  2.51 us (7%)
    pallas_call x4, Pallas kernels, call(): pl.pallas_call(kernel, grid=(1,) if form == 'block' else (), in_specs=[fr...  14.4 us
    ppermute x1, starting transfers between devices, per_device(): right = lax.ppermute(to_left, axes, [(b, a) for a, b in steps])  6.03 us
    ppermute x3, starting transfers between devices, across(): return lax.ppermute(values, axes, pairs)  4.73 us
    all_to_all x1, starting transfers between devices, per_device(): lax.all_to_all(rows_out, 'tile', split_axis=0, concat_axis=0, tiled=True)  3.87 us
    all_to_all x1, waiting for transfers between devices, per_device(): lax.all_to_all(rows_out, 'tile', split_axis=0, concat_axis=0, tiled=True)  2.5 us
    pallas_call x1, Pallas kernels, per_device(): pl.pallas_call(out_kernel, grid=(1,), in_specs=[pl.BlockSpec((fields, 8,...  2.36 us
    ppermute x1, starting transfers between devices, per_device(): left = lax.ppermute(to_right, axes, steps)  1.11 us
  transfers between devices with their start and end apart: 6, of which 1 were waited for; matrix products, arithmetic and copies ran while one was open for 0% of the time, Pallas kernels for 30%

profile of v4, /device:TPU:1, one launch (start us, length us, event | category | flops | bytes accessed | tf_op | source)
XLA Modules:
  0.0 35.3 jit_solution(15896558543065091733)
XLA Ops:
  0.0 0.0 copy-start
  0.0 0.0 copy-start.5
  0.0 0.0 copy-start.6
  0.0 2.4 %shard_map.92 = f32[32,4,128]{2,1,0:T(4,128)} custom-call(f32[3,64,2048]{2,1,0:T(8,128)} %bitcast.11, s32[32,2,128]{2,1,0:T(2,128)} %bitcast.20, f32[32,128]{1,0:T(8,128)} %bitcast.21), custom_call_target="tpu_custom_call" | custom-call | tf_op jit(solution)/shard_map/pallas_call | solution.py:389
  2.4 4.3 %collective-permute-start = (f32[32,4,128]{2,1,0:T(4,128)}, f32[32,4,128]{2,1,0:T(4,128)S(1)}, u32[]{:S(2)}, u32[]{:S(2)}) collective-permute-start(f32[32,4,128]{2,1,0:T(4,128)} %shard_map.92), channel_id=1, source_target_pairs={{0,96},{1,97},{2,98},{3,99},{4,100},{5,101},{6,102},{7,103},{8,104... | collective-permute-start | bytes 196616 | tf_op jit(solution)/shard_map/ppermute | solution.py:403
  6.7 0.0 collective-permute-start.1
  6.7 0.4 %collective-permute-start.2 = (f32[32,4,128]{2,1,0:T(4,128)}, f32[32,4,128]{2,1,0:T(4,128)S(1)}, u32[]{:S(2)}, u32[]{:S(2)}) collective-permute-start(f32[32,4,128]{2,1,0:T(4,128)} %shard_map.92), channel_id=1, source_target_pairs={{0,32},{1,33},{2,34},{3,35},{4,36},{5,37},{6,38},{7,39},{8,40},{9,... | collective-permute-start | bytes 196616 | tf_op jit(solution)/shard_map/ppermute | solution.py:403
  7.1 0.0 copy-done
  7.1 0.0 copy-done.5
  7.1 0.0 copy-done.6
  7.1 0.0 copy-start.1
  7.1 0.0 copy-start.2
  7.1 0.0 copy-start.3
  7.1 0.0 copy-start.4
  7.2 3.0 %shard_map.91 = (f32[192,2048]{1,0:T(8,128)S(1)}, f32[192,128]{1,0:T(8,128)S(1)}, f32[192,128]{1,0:T(8,128)S(1)}) custom-call(f32[192,2048]{1,0:T(8,128)S(1)} %bitcast.12, f32[1,2048]{1,0:T(1,128)S(1)} %bitcast.17, s32[2,128]{1,0:T(2,128)S(1)} %bitcast.19), custom_call_target="tpu_custom_call" | custom-call | flops 4000000000 | bytes 4000000 | tf_op jit(solution)/shard_map/pallas_call | solution.py:353
  10.2 1.1 %collective-permute-start.3 = (f32[192,128]{1,0:T(8,128)S(1)}, f32[192,128]{1,0:T(8,128)S(1)}, u32[]{:S(2)}, u32[]{:S(2)}) collective-permute-start(f32[192,128]{1,0:T(8,128)S(1)} %get-tuple-element.13.after), channel_id=1, source_target_pairs={{0,1},{1,2},{2,3},{3,4},{4,5},{5,6},{6,7},{7,8},{8,9},{9,10},{10,1... | collective-permute-start | bytes 294920 | tf_op jit(solution)/shard_map/ppermute | solution.py:419
  11.3 6.0 %collective-permute-start.4 = (f32[192,128]{1,0:T(8,128)S(1)}, f32[192,128]{1,0:T(8,128)S(1)}, u32[]{:S(2)}, u32[]{:S(2)}) collective-permute-start(f32[192,128]{1,0:T(8,128)S(1)} %get-tuple-element.15), channel_id=1, source_target_pairs={{1,0},{2,1},{3,2},{4,3},{5,4},{6,5},{7,6},{8,7},{9,8},{10,9},{11,1... | collective-permute-start | bytes 294920 | tf_op jit(solution)/shard_map/ppermute | solution.py:420
  17.3 0.0 collective-permute-done.got0
  17.3 0.0 collective-permute-done.1.got1
  17.3 0.0 collective-permute-done.2.got2
  17.3 0.0 copy-done.1
  17.3 0.0 copy-done.2
  17.3 1.4 %shard_map.93.after = f32[32,12,128]{2,1,0:T(8,128)} custom-call(f32[32,4,128]{2,1,0:T(4,128)S(1)} %collective-permute-done.got0, f32[32,4,128]{2,1,0:T(4,128)S(1)} %collective-permute-done.1.got1, f32[32,4,128]{2,1,0:T(4,128)S(1)} %collective-permute-done.2.got2, s32[32,2,128]{2,1,0:T(2,128)S(1)} %bitcast.13, f32[32,128]{1,0:T(8,128)S(1)} %bitcast.14, ...), custom_call_target="tpu_custom_call" | custom-call | tf_op jit(solution)/shard_map/pallas_call | solution.py:353
  18.8 3.9 %all-to-all-start = ((f32[32,12,128]{2,1,0:T(8,128)}), f32[32,12,128]{2,1,0:T(8,128)S(1)}, u32[]{:S(2)}, u32[]{:S(2)}) async-start(f32[32,12,128]{2,1,0:T(8,128)} %shard_map.93.after), calls=%async_computation | async-start | bytes 524288 | tf_op jit(solution)/shard_map/all_to_all | solution.py:427
  22.7 0.0 copy-done.3
  22.7 0.0 copy-done.4
  22.7 6.3 %shard_map.94 = (f32[192,2048]{1,0:T(8,128)S(1)}, f32[1,2048]{1,0:T(1,128)S(1)}, s32[6,1,2048]{2,1,0:T(1,128)S(1)}, f32[64,64]{1,0:T(8,128)S(1)}) custom-call(f32[192,2048]{1,0:T(8,128)S(1)} %get-tuple-element.12.state, f32[1,2048]{1,0:T(1,128)S(1)} %bitcast.18, s32[6,1,2048]{2,1,0:T(1,128)S(1)} %bitcast.15, ...), custom_call_target="tpu_custom_call", output_to_operand_aliasing={{0}: (0, {})} | custom-call | flops 8000000000 | bytes 4000000 | tf_op jit(solution)/shard_map/pallas_call | solution.py:353
  29.0 0.0 collective-permute-done.3.left
  29.0 0.0 collective-permute-done.4.right
  29.0 2.5 %all-to-all-done.got = f32[32,12,128]{2,1,0:T(8,128)S(1)} async-done(((f32[32,12,128]{2,1,0:T(8,128)}), f32[32,12,128]{2,1,0:T(8,128)S(1)}, u32[]{:S(2)}, u32[]{:S(2)}) %all-to-all-start) | async-done | bytes 196640 | tf_op jit(solution)/shard_map/all_to_all | solution.py:427
  31.5 3.7 %shard_map.95 = f32[192,2048]{1,0:T(8,128)} custom-call(f32[192,2048]{1,0:T(8,128)S(1)} %get-tuple-element.14.partial, f32[192,128]{1,0:T(8,128)S(1)} %collective-permute-done.3.left, f32[192,128]{1,0:T(8,128)S(1)} %collective-permute-done.4.right, f32[32,12,128]{2,1,0:T(8,128)S(1)} %all-to-all-done.got, f32[1,2048]{1,0:T(1,128)S(1)} %get-tuple-element.16.gains, ...), custom_call_target="tpu_custom_call" | custom-call | tf_op jit(solution)/shard_map/pallas_call | solution.py:353
Async XLA Ops:
  0.0 7.1 %copy-start = (f32[1,1,3,64,2048]{4,3,2,1,0:T(8,128)S(1)}, f32[1,1,3,64,2048]{4,3,2,1,0:T(8,128)}, u32[]{:S(2)}) copy-start(f32[1,1,3,64,2048]{4,3,2,1,0:T(8,128)} %param.9) | copy-start | bytes 4718596
  0.0 7.1 %copy-start.5 = (f32[1,1,2048]{2,1,0:T(1,128)S(1)}, f32[1,1,2048]{2,1,0:T(1,128)}, u32[]{:S(2)}) copy-start(f32[1,1,2048]{2,1,0:T(1,128)} %param.10) | copy-start | bytes 24580
  0.0 7.1 %copy-start.6 = (s32[1,1,2,128]{3,2,1,0:T(2,128)S(1)}, s32[1,1,2,128]{3,2,1,0:T(2,128)}, u32[]{:S(2)}) copy-start(s32[1,1,2,128]{3,2,1,0:T(2,128)} %param.13) | copy-start | bytes 3076
  2.4 14.9 %collective-permute-start = (f32[32,4,128]{2,1,0:T(4,128)}, f32[32,4,128]{2,1,0:T(4,128)S(1)}, u32[]{:S(2)}, u32[]{:S(2)}) collective-permute-start(f32[32,4,128]{2,1,0:T(4,128)} %shard_map.92), channel_id=1, source_target_pairs={{0,96},{1,97},{2,98},{3,99},{4,100},{5,101},{6,102},{7,103},{8,104... | collective-permute-start | bytes 196616 | tf_op jit(solution)/shard_map/ppermute | solution.py:403
  6.7 10.6 %collective-permute-start.1 = (f32[32,4,128]{2,1,0:T(4,128)}, f32[32,4,128]{2,1,0:T(4,128)S(1)}, u32[]{:S(2)}, u32[]{:S(2)}) collective-permute-start(f32[32,4,128]{2,1,0:T(4,128)} %shard_map.92), channel_id=1, source_target_pairs={{0,64},{1,65},{2,66},{3,67},{4,68},{5,69},{6,70},{7,71},{8,72},{9,... | collective-permute-start | bytes 196616 | tf_op jit(solution)/shard_map/ppermute | solution.py:403
  6.7 10.6 %collective-permute-start.2 = (f32[32,4,128]{2,1,0:T(4,128)}, f32[32,4,128]{2,1,0:T(4,128)S(1)}, u32[]{:S(2)}, u32[]{:S(2)}) collective-permute-start(f32[32,4,128]{2,1,0:T(4,128)} %shard_map.92), channel_id=1, source_target_pairs={{0,32},{1,33},{2,34},{3,35},{4,36},{5,37},{6,38},{7,39},{8,40},{9,... | collective-permute-start | bytes 196616 | tf_op jit(solution)/shard_map/ppermute | solution.py:403
  7.1 10.2 %copy-start.1 = (s32[1,1,32,2,128]{4,3,2,1,0:T(2,128)S(1)}, s32[1,1,32,2,128]{4,3,2,1,0:T(2,128)}, u32[]{:S(2)}) copy-start(s32[1,1,32,2,128]{4,3,2,1,0:T(2,128)} %param.16) | copy-start | bytes 98308
  7.1 10.2 %copy-start.2 = (f32[1,1,32,128]{3,2,1,0:T(8,128)S(1)}, f32[1,1,32,128]{3,2,1,0:T(8,128)}, u32[]{:S(2)}) copy-start(f32[1,1,32,128]{3,2,1,0:T(8,128)} %param.17) | copy-start | bytes 49156
  7.1 15.5 %copy-start.3 = (s32[1,1,6,2048]{3,1,2,0:T(1,128)S(1)}, s32[1,1,6,2048]{3,1,2,0:T(1,128)}, u32[]{:S(2)}) copy-start(s32[1,1,6,2048]{3,1,2,0:T(1,128)} %param.12) | copy-start | bytes 147460
  7.1 15.5 %copy-start.4 = (f32[1,64,64]{2,1,0:T(8,128)S(1)}, f32[1,64,64]{2,1,0:T(8,128)}, u32[]{:S(2)}) copy-start(f32[1,64,64]{2,1,0:T(8,128)} %param.11) | copy-start | bytes 49156
  10.2 18.8 %collective-permute-start.3 = (f32[192,128]{1,0:T(8,128)S(1)}, f32[192,128]{1,0:T(8,128)S(1)}, u32[]{:S(2)}, u32[]{:S(2)}) collective-permute-start(f32[192,128]{1,0:T(8,128)S(1)} %get-tuple-element.13.after), channel_id=1, source_target_pairs={{0,1},{1,2},{2,3},{3,4},{4,5},{5,6},{6,7},{7,8},{8,9},{9,10},{10,1... | collective-permute-start | bytes 294920 | tf_op jit(solution)/shard_map/ppermute | solution.py:419
  11.3 17.7 %collective-permute-start.4 = (f32[192,128]{1,0:T(8,128)S(1)}, f32[192,128]{1,0:T(8,128)S(1)}, u32[]{:S(2)}, u32[]{:S(2)}) collective-permute-start(f32[192,128]{1,0:T(8,128)S(1)} %get-tuple-element.15), channel_id=1, source_target_pairs={{1,0},{2,1},{3,2},{4,3},{5,4},{6,5},{7,6},{8,7},{9,8},{10,9},{11,1... | collective-permute-start | bytes 294920 | tf_op jit(solution)/shard_map/ppermute | solution.py:420
  18.8 12.7 %all-to-all-start = ((f32[32,12,128]{2,1,0:T(8,128)}), f32[32,12,128]{2,1,0:T(8,128)S(1)}, u32[]{:S(2)}, u32[]{:S(2)}) async-start(f32[32,12,128]{2,1,0:T(8,128)} %shard_map.93.after), calls=%async_computation | async-start | bytes 524288 | tf_op jit(solution)/shard_map/all_to_all | solution.py:427

commit v5 on v4

--- a/solution.py
+++ b/solution.py
@@ -250,9 +250,7 @@
         run(6, True)
 
 
-def final_kernel(
-    partial, left, right, got, gains, links, column, result, done, rim_parts, left_rows, onehots, count, wide, sems
-):
+def rim_kernel(partial, left, right, gains, links, column, mixed, column_out, rim_parts, count, wide):
     comp = lax.axis_index("comp")
     tile = lax.axis_index("tile")
     last_comp = lax.axis_size("comp") - 1
@@ -262,8 +260,47 @@
     has_right = jnp.logical_not((tile == last_tile) & (comp >= last_comp - 1))
     rows, nodes = partial.shape
     levels = column.shape[0]
+    rim = left.shape[1]
+    width = 2 * LANES
+    chunks = nodes // LANES
+    column_out[...] = column[...]
+    for side, there, source in ((0, has_left, left), (1, has_right, right)):
+        high, low = split(jnp.where(there, source[...], 0.0))
+        rim_parts[0:rows, side * rim : (side + 1) * rim] = high
+        rim_parts[rows:, side * rim : (side + 1) * rim] = low
+    wide[...] = jnp.zeros(wide.shape, F32)
+    for f in range(rows // levels):
+        at = f * levels
+        wide[at : at + levels, at : at + levels] = column[...]
+    col_high, col_low = split(wide[:, 0:rows])
+    col = jnp.concatenate([col_high, col_low], axis=0)
+
+    def run(used):
+        for at in range(nodes // width):
+            where = slice(at * width, (at + 1) * width)
+            here = count.at[at % 2]
+            count_links([links[k, :, where] for k in range(used)], [0, chunks + 1], here)
+            both = dot(rim_parts[...], here[...])
+            updated = partial[:, where] + gains[0:1, where] * (both[:rows] + both[rows:])
+            high, low = split(updated)
+            full = dot(col, high)
+            mixed[:, where] = full[:rows] + full[rows:] + dot(col_high, low)
+
+    @pl.when(jnp.logical_not(ocean))
+    def _():
+        run(3)
+
+    @pl.when(ocean)
+    def _():
+        run(6)
+
+
+def final_kernel(mixed, got, column, result, done, left_rows, onehots, sems):
+    last_comp = lax.axis_size("comp") - 1
+    ocean = lax.axis_index("comp") == last_comp
+    rows, nodes = mixed.shape
+    levels = column.shape[0]
     senders = got.shape[0]
-    rim = left.shape[1]
     width = 2 * LANES
     tiles = nodes // width
     fields = rows // levels
@@ -295,46 +332,20 @@
     landed = lax.fori_loop(0, groups, land, jnp.zeros((2 * fields * chunks, LANES), F32))
     forcing = COUPLING * (landed[: fields * chunks] + landed[fields * chunks :])
 
-    for side, there, source in ((0, has_left, left), (1, has_right, right)):
-        high, low = split(jnp.where(there, source[...], 0.0))
-        rim_parts[0:rows, side * rim : (side + 1) * rim] = high
-        rim_parts[rows:, side * rim : (side + 1) * rim] = low
-    wide[...] = jnp.zeros(wide.shape, F32)
-    for f in range(fields):
-        at = f * levels
-        wide[at : at + levels, at : at + levels] = column[...]
-    col_high, col_low = split(wide[:, 0:rows])
-    col = jnp.concatenate([col_high, col_low], axis=0)
-    col_gain = column[:, 0:1]
+    col_gain = jnp.broadcast_to(column[:, 0:1], (levels, width))
 
     def move(at):
         where = pl.ds(at * width, width)
         return pltpu.make_async_copy(done.at[:, where], result.at[:, where], sems.at[at])
 
-    def run(used):
-        for at in range(tiles):
-            where = slice(at * width, (at + 1) * width)
-            here = count.at[at % 2]
-            count_links([links[k, :, where] for k in range(used)], [0, chunks + 1], here)
-            both = dot(rim_parts[...], here[...])
-            updated = partial[:, where] + gains[0:1, where] * (both[:rows] + both[rows:])
-            high, low = split(updated)
-            full = dot(col, high)
-            mixed = full[:rows] + full[rows:] + dot(col_high, low)
-            for f in range(fields):
-                part = slice(f * levels, (f + 1) * levels)
-                first = f * chunks + at * width // LANES
-                rows_of = [forcing[n : n + 1, :] for n in range(first, first + width // LANES)]
-                done[part, where] = mixed[part] + col_gain * jnp.concatenate(rows_of, axis=1)
-            move(at).start()
-
-    @pl.when(jnp.logical_not(ocean))
-    def _():
-        run(3)
-
-    @pl.when(ocean)
-    def _():
-        run(6)
+    for at in range(tiles):
+        where = slice(at * width, (at + 1) * width)
+        for f in range(fields):
+            part = slice(f * levels, (f + 1) * levels)
+            first = f * chunks + at * width // LANES
+            rows_of = [forcing[n : n + 1, :] for n in range(first, first + width // LANES)]
+            done[part, where] = mixed[part, where] + col_gain * jnp.concatenate(rows_of, axis=1)
+        move(at).start()
 
     for at in range(tiles):
         move(at).wait()
@@ -430,22 +441,26 @@
         inner_kernel,
         (state_here, metric_row, link_rows, column_op.reshape(levels, levels), rows_out),
         [shape(rows, nodes), shape(1, nodes), shape(6, 1, nodes, kind=int32), shape(levels, levels)],
-        [held(2, nodes, width, kind=BF), held(2 * rows, nodes, kind=BF), held(3 * LANES, 3 * LANES, kind=BF)],
+        [held(4, nodes, width, kind=BF), held(2 * rows, nodes, kind=BF), held(3 * LANES, 3 * LANES, kind=BF)],
         anywhere=(4,),
         cost=8_000_000_000,
         alias={0: 0},
     )
+    mixed, column = call(
+        rim_kernel,
+        (partial, left, right, gains, links_here, column),
+        [shape(rows, nodes), shape(levels, levels)],
+        [held(2 * rows, 2 * rim, kind=BF), held(2, 2 * rim, width, kind=BF), held(rows, width)],
+        alias={0: 0},
+    )
     (result,) = call(
         final_kernel,
-        (partial, left, right, got, gains, links_here, column),
+        (mixed, got, column),
         [shape(rows, nodes)],
         [
             held(rows, nodes),
-            held(2 * rows, 2 * rim, kind=BF),
             held(2 * fields * chunks, ntile * slot, kind=BF),
             held(LANES, ntile * slot, kind=BF),
-            held(2, 2 * rim, width, kind=BF),
-            held(rows, width),
             dma((tiles,)),
         ],
         out_far=(0,),

time: 35.5 us -> 33.9 us (0.955)
  waiting for transfers between devices: 2.51 us -> 0.73 us
    all_to_all x1, waiting for transfers between devices: 2.5 us -> 0.72 us  [per_device(): lax.all_to_all(rows_out, 'tile', split_axis=0, concat_axis=0, tiled=True)]
    pallas_call x4 -> x5, Pallas kernels: 14.4 us -> 14.5 us  [call(): pl.pallas_call(kernel, grid=(1,) if form == 'block' else (), in_specs=[fr...]
  transfers between devices with their start and end apart: 6 -> 6, of which waited for: 1 -> 1; matrix products, arithmetic and copies ran while one was open for 0% -> 0% of each run, Pallas kernels for 30% -> 37%
where the time goes in v5:
time: 33.9 us; the launch traced here: 33.7 us
  Pallas kernels  16.9 us (50%)
  starting transfers between devices  15.7 us (46%)
  waiting for transfers between devices  0.73 us (2%)
    pallas_call x5, Pallas kernels, call(): pl.pallas_call(kernel, grid=(1,) if form == 'block' else (), in_specs=[fr...  14.5 us
    ppermute x1, starting transfers between devices, per_device(): right = lax.ppermute(to_left, axes, [(b, a) for a, b in steps])  6.03 us
    ppermute x3, starting transfers between devices, across(): return lax.ppermute(values, axes, pairs)  4.73 us
    all_to_all x1, starting transfers between devices, per_device(): lax.all_to_all(rows_out, 'tile', split_axis=0, concat_axis=0, tiled=True)  3.87 us
    pallas_call x1, Pallas kernels, per_device(): pl.pallas_call(out_kernel, grid=(1,), in_specs=[pl.BlockSpec((fields, 8,...  2.36 us
    ppermute x1, starting transfers between devices, per_device(): left = lax.ppermute(to_right, axes, steps)  1.11 us
    all_to_all x1, waiting for transfers between devices, per_device(): lax.all_to_all(rows_out, 'tile', split_axis=0, concat_axis=0, tiled=True)  0.72 us
  transfers between devices with their start and end apart: 6, of which 1 were waited for; matrix products, arithmetic and copies ran while one was open for 0% of the time, Pallas kernels for 37%

profile of v5, /device:TPU:1, one launch (start us, length us, event | category | flops | bytes accessed | tf_op | source)
XLA Modules:
  0.0 33.7 jit_solution(17284332609097467492)
XLA Ops:
  0.0 0.0 copy-start
  0.0 0.0 copy-start.5
  0.0 0.0 copy-start.6
  0.0 2.4 %shard_map.92 = f32[32,4,128]{2,1,0:T(4,128)} custom-call(f32[3,64,2048]{2,1,0:T(8,128)} %bitcast.11, s32[32,2,128]{2,1,0:T(2,128)} %bitcast.20, f32[32,128]{1,0:T(8,128)} %bitcast.21), custom_call_target="tpu_custom_call" | custom-call | tf_op jit(solution)/shard_map/pallas_call | solution.py:400
  2.4 4.3 %collective-permute-start = (f32[32,4,128]{2,1,0:T(4,128)}, f32[32,4,128]{2,1,0:T(4,128)S(1)}, u32[]{:S(2)}, u32[]{:S(2)}) collective-permute-start(f32[32,4,128]{2,1,0:T(4,128)} %shard_map.92), channel_id=1, source_target_pairs={{0,96},{1,97},{2,98},{3,99},{4,100},{5,101},{6,102},{7,103},{8,104... | collective-permute-start | bytes 196616 | tf_op jit(solution)/shard_map/ppermute | solution.py:414
  6.7 0.0 collective-permute-start.1
  6.7 0.4 %collective-permute-start.2 = (f32[32,4,128]{2,1,0:T(4,128)}, f32[32,4,128]{2,1,0:T(4,128)S(1)}, u32[]{:S(2)}, u32[]{:S(2)}) collective-permute-start(f32[32,4,128]{2,1,0:T(4,128)} %shard_map.92), channel_id=1, source_target_pairs={{0,32},{1,33},{2,34},{3,35},{4,36},{5,37},{6,38},{7,39},{8,40},{9,... | collective-permute-start | bytes 196616 | tf_op jit(solution)/shard_map/ppermute | solution.py:414
  7.1 0.0 copy-done
  7.1 0.0 copy-done.5
  7.1 0.0 copy-done.6
  7.1 0.0 copy-start.1
  7.1 0.0 copy-start.2
  7.1 0.0 copy-start.3
  7.1 0.0 copy-start.4
  7.2 3.0 %shard_map.91 = (f32[192,2048]{1,0:T(8,128)S(1)}, f32[192,128]{1,0:T(8,128)S(1)}, f32[192,128]{1,0:T(8,128)S(1)}) custom-call(f32[192,2048]{1,0:T(8,128)S(1)} %bitcast.12, f32[1,2048]{1,0:T(1,128)S(1)} %bitcast.17, s32[2,128]{1,0:T(2,128)S(1)} %bitcast.19), custom_call_target="tpu_custom_call" | custom-call | flops 4000000000 | bytes 4000000 | tf_op jit(solution)/shard_map/pallas_call | solution.py:364
  10.2 1.1 %collective-permute-start.3 = (f32[192,128]{1,0:T(8,128)S(1)}, f32[192,128]{1,0:T(8,128)S(1)}, u32[]{:S(2)}, u32[]{:S(2)}) collective-permute-start(f32[192,128]{1,0:T(8,128)S(1)} %get-tuple-element.15.after), channel_id=1, source_target_pairs={{0,1},{1,2},{2,3},{3,4},{4,5},{5,6},{6,7},{7,8},{8,9},{9,10},{10,1... | collective-permute-start | bytes 294920 | tf_op jit(solution)/shard_map/ppermute | solution.py:430
  11.3 6.0 %collective-permute-start.4 = (f32[192,128]{1,0:T(8,128)S(1)}, f32[192,128]{1,0:T(8,128)S(1)}, u32[]{:S(2)}, u32[]{:S(2)}) collective-permute-start(f32[192,128]{1,0:T(8,128)S(1)} %get-tuple-element.17), channel_id=1, source_target_pairs={{1,0},{2,1},{3,2},{4,3},{5,4},{6,5},{7,6},{8,7},{9,8},{10,9},{11,1... | collective-permute-start | bytes 294920 | tf_op jit(solution)/shard_map/ppermute | solution.py:431
  17.3 0.0 collective-permute-done.got0
  17.3 0.0 collective-permute-done.1.got1
  17.3 0.0 collective-permute-done.2.got2
  17.3 0.0 copy-done.1
  17.3 0.0 copy-done.2
  17.3 1.4 %shard_map.93.after = f32[32,12,128]{2,1,0:T(8,128)} custom-call(f32[32,4,128]{2,1,0:T(4,128)S(1)} %collective-permute-done.got0, f32[32,4,128]{2,1,0:T(4,128)S(1)} %collective-permute-done.1.got1, f32[32,4,128]{2,1,0:T(4,128)S(1)} %collective-permute-done.2.got2, s32[32,2,128]{2,1,0:T(2,128)S(1)} %bitcast.13, f32[32,128]{1,0:T(8,128)S(1)} %bitcast.14, ...), custom_call_target="tpu_custom_call" | custom-call | tf_op jit(solution)/shard_map/pallas_call | solution.py:364
  18.8 3.9 %all-to-all-start = ((f32[32,12,128]{2,1,0:T(8,128)}), f32[32,12,128]{2,1,0:T(8,128)S(1)}, u32[]{:S(2)}, u32[]{:S(2)}) async-start(f32[32,12,128]{2,1,0:T(8,128)} %shard_map.93.after), calls=%async_computation | async-start | bytes 524288 | tf_op jit(solution)/shard_map/all_to_all | solution.py:438
  22.7 0.0 copy-done.3
  22.7 0.0 copy-done.4
  22.7 6.1 %shard_map.94 = (f32[192,2048]{1,0:T(8,128)S(1)}, f32[1,2048]{1,0:T(1,128)S(1)}, s32[6,1,2048]{2,1,0:T(1,128)S(1)}, f32[64,64]{1,0:T(8,128)S(1)}) custom-call(f32[192,2048]{1,0:T(8,128)S(1)} %get-tuple-element.14.state, f32[1,2048]{1,0:T(1,128)S(1)} %bitcast.18, s32[6,1,2048]{2,1,0:T(1,128)S(1)} %bitcast.15, ...), custom_call_target="tpu_custom_call", output_to_operand_aliasing={{0}: (0, {})} | custom-call | flops 8000000000 | bytes 4000000 | tf_op jit(solution)/shard_map/pallas_call | solution.py:364
  28.8 0.0 collective-permute-done.3.left
  28.8 0.0 collective-permute-done.4.right
  28.8 2.0 %shard_map.95 = (f32[192,2048]{1,0:T(8,128)S(1)}, f32[64,64]{1,0:T(8,128)S(1)}) custom-call(f32[192,2048]{1,0:T(8,128)S(1)} %get-tuple-element.16.partial, f32[192,128]{1,0:T(8,128)S(1)} %collective-permute-done.3.left, f32[192,128]{1,0:T(8,128)S(1)} %collective-permute-done.4.right, ...), custom_call_target="tpu_custom_call", output_to_operand_aliasing={{0}: (0, {})} | custom-call | tf_op jit(solution)/shard_map/pallas_call | solution.py:364
  30.8 0.7 %all-to-all-done.got = f32[32,12,128]{2,1,0:T(8,128)S(1)} async-done(((f32[32,12,128]{2,1,0:T(8,128)}), f32[32,12,128]{2,1,0:T(8,128)S(1)}, u32[]{:S(2)}, u32[]{:S(2)}) %all-to-all-start) | async-done | bytes 196640 | tf_op jit(solution)/shard_map/all_to_all | solution.py:438
  31.5 2.0 %shard_map.96 = f32[192,2048]{1,0:T(8,128)} custom-call(f32[192,2048]{1,0:T(8,128)S(1)} %get-tuple-element.21.mixed, f32[32,12,128]{2,1,0:T(8,128)S(1)} %all-to-all-done.got, f32[64,64]{1,0:T(8,128)S(1)} %get-tuple-element.22.column), custom_call_target="tpu_custom_call" | custom-call | tf_op jit(solution)/shard_map/pallas_call | solution.py:364
Async XLA Ops:
  0.0 7.1 %copy-start = (f32[1,1,3,64,2048]{4,3,2,1,0:T(8,128)S(1)}, f32[1,1,3,64,2048]{4,3,2,1,0:T(8,128)}, u32[]{:S(2)}) copy-start(f32[1,1,3,64,2048]{4,3,2,1,0:T(8,128)} %param.9) | copy-start | bytes 4718596
  0.0 7.1 %copy-start.5 = (f32[1,1,2048]{2,1,0:T(1,128)S(1)}, f32[1,1,2048]{2,1,0:T(1,128)}, u32[]{:S(2)}) copy-start(f32[1,1,2048]{2,1,0:T(1,128)} %param.10) | copy-start | bytes 24580
  0.0 7.1 %copy-start.6 = (s32[1,1,2,128]{3,2,1,0:T(2,128)S(1)}, s32[1,1,2,128]{3,2,1,0:T(2,128)}, u32[]{:S(2)}) copy-start(s32[1,1,2,128]{3,2,1,0:T(2,128)} %param.13) | copy-start | bytes 3076
  2.4 14.9 %collective-permute-start = (f32[32,4,128]{2,1,0:T(4,128)}, f32[32,4,128]{2,1,0:T(4,128)S(1)}, u32[]{:S(2)}, u32[]{:S(2)}) collective-permute-start(f32[32,4,128]{2,1,0:T(4,128)} %shard_map.92), channel_id=1, source_target_pairs={{0,96},{1,97},{2,98},{3,99},{4,100},{5,101},{6,102},{7,103},{8,104... | collective-permute-start | bytes 196616 | tf_op jit(solution)/shard_map/ppermute | solution.py:414
  6.7 10.6 %collective-permute-start.1 = (f32[32,4,128]{2,1,0:T(4,128)}, f32[32,4,128]{2,1,0:T(4,128)S(1)}, u32[]{:S(2)}, u32[]{:S(2)}) collective-permute-start(f32[32,4,128]{2,1,0:T(4,128)} %shard_map.92), channel_id=1, source_target_pairs={{0,64},{1,65},{2,66},{3,67},{4,68},{5,69},{6,70},{7,71},{8,72},{9,... | collective-permute-start | bytes 196616 | tf_op jit(solution)/shard_map/ppermute | solution.py:414
  6.7 10.6 %collective-permute-start.2 = (f32[32,4,128]{2,1,0:T(4,128)}, f32[32,4,128]{2,1,0:T(4,128)S(1)}, u32[]{:S(2)}, u32[]{:S(2)}) collective-permute-start(f32[32,4,128]{2,1,0:T(4,128)} %shard_map.92), channel_id=1, source_target_pairs={{0,32},{1,33},{2,34},{3,35},{4,36},{5,37},{6,38},{7,39},{8,40},{9,... | collective-permute-start | bytes 196616 | tf_op jit(solution)/shard_map/ppermute | solution.py:414
  7.1 10.2 %copy-start.1 = (s32[1,1,32,2,128]{4,3,2,1,0:T(2,128)S(1)}, s32[1,1,32,2,128]{4,3,2,1,0:T(2,128)}, u32[]{:S(2)}) copy-start(s32[1,1,32,2,128]{4,3,2,1,0:T(2,128)} %param.16) | copy-start | bytes 98308
  7.1 10.2 %copy-start.2 = (f32[1,1,32,128]{3,2,1,0:T(8,128)S(1)}, f32[1,1,32,128]{3,2,1,0:T(8,128)}, u32[]{:S(2)}) copy-start(f32[1,1,32,128]{3,2,1,0:T(8,128)} %param.17) | copy-start | bytes 49156
  7.1 15.5 %copy-start.3 = (s32[1,1,6,2048]{3,1,2,0:T(1,128)S(1)}, s32[1,1,6,2048]{3,1,2,0:T(1,128)}, u32[]{:S(2)}) copy-start(s32[1,1,6,2048]{3,1,2,0:T(1,128)} %param.12) | copy-start | bytes 147460
  7.1 15.5 %copy-start.4 = (f32[1,64,64]{2,1,0:T(8,128)S(1)}, f32[1,64,64]{2,1,0:T(8,128)}, u32[]{:S(2)}) copy-start(f32[1,64,64]{2,1,0:T(8,128)} %param.11) | copy-start | bytes 49156
  10.2 18.6 %collective-permute-start.3 = (f32[192,128]{1,0:T(8,128)S(1)}, f32[192,128]{1,0:T(8,128)S(1)}, u32[]{:S(2)}, u32[]{:S(2)}) collective-permute-start(f32[192,128]{1,0:T(8,128)S(1)} %get-tuple-element.15.after), channel_id=1, source_target_pairs={{0,1},{1,2},{2,3},{3,4},{4,5},{5,6},{6,7},{7,8},{8,9},{9,10},{10,1... | collective-permute-start | bytes 294920 | tf_op jit(solution)/shard_map/ppermute | solution.py:430
  11.3 17.5 %collective-permute-start.4 = (f32[192,128]{1,0:T(8,128)S(1)}, f32[192,128]{1,0:T(8,128)S(1)}, u32[]{:S(2)}, u32[]{:S(2)}) collective-permute-start(f32[192,128]{1,0:T(8,128)S(1)} %get-tuple-element.17), channel_id=1, source_target_pairs={{1,0},{2,1},{3,2},{4,3},{5,4},{6,5},{7,6},{8,7},{9,8},{10,9},{11,1... | collective-permute-start | bytes 294920 | tf_op jit(solution)/shard_map/ppermute | solution.py:431
  18.8 12.7 %all-to-all-start = ((f32[32,12,128]{2,1,0:T(8,128)}), f32[32,12,128]{2,1,0:T(8,128)S(1)}, u32[]{:S(2)}, u32[]{:S(2)}) async-start(f32[32,12,128]{2,1,0:T(8,128)} %shard_map.93.after), calls=%async_computation | async-start | bytes 524288 | tf_op jit(solution)/shard_map/all_to_all | solution.py:438

commit v6 on v5

--- a/solution.py
+++ b/solution.py
@@ -136,9 +136,10 @@
 def pick_rims(wanted, parts):
     nodes = parts.shape[1]
     rows = parts.shape[0] // 2
-    ids = lax.broadcasted_iota(jnp.int16, (nodes, LANES), 0)
-    wanted = jnp.broadcast_to(wanted, (16, LANES)).astype(jnp.int16)
-    wanted = jnp.broadcast_to(wanted[None], (nodes // 16, 16, LANES)).reshape(nodes, LANES)
+    many = wanted.shape[1]
+    ids = lax.broadcasted_iota(jnp.int16, (nodes, many), 0)
+    wanted = jnp.broadcast_to(wanted, (16, many)).astype(jnp.int16)
+    wanted = jnp.broadcast_to(wanted[None], (nodes // 16, 16, many)).reshape(nodes, many)
     onehot = jnp.where(ids == wanted, jnp.ones((), BF), jnp.zeros((), BF))
     both = dot(parts[...], onehot)
     return both[:rows] + both[rows:]
@@ -204,8 +205,10 @@
 def field_kernel(state, metric, rims, state_here, left_ref, right_ref, parts, tables):
     state_here[...] = state[...]
     fill_parts(lax.axis_index("comp") != lax.axis_size("comp") - 1, state, metric, parts, tables)
-    left_ref[...] = pick_rims(rims[0:1, :], parts)
-    right_ref[...] = pick_rims(rims[1:2, :], parts)
+    rim = rims.shape[1]
+    sides = pick_rims(jnp.concatenate([rims[0:1, :], rims[1:2, :]], axis=1), parts)
+    left_ref[...] = sides[:, :rim]
+    right_ref[...] = sides[:, rim:]
 
 
 def inner_kernel(state, metric, links, column, after, partial, gains, links_out, column_out, count, parts, tables):

time: 33.9 us -> 33.5 us (0.988)
  Pallas kernels: 16.9 us -> 16.5 us
    pallas_call x5, Pallas kernels: 14.5 us -> 14.1 us  [call(): pl.pallas_call(kernel, grid=(1,) if form == 'block' else (), in_specs=[fr...]
  transfers between devices with their start and end apart: 6 -> 6, of which waited for: 1 -> 1; matrix products, arithmetic and copies ran while one was open for 0% -> 0% of each run, Pallas kernels for 37% -> 36%
where the time goes in v6:
time: 33.5 us; the launch traced here: 33.3 us
  Pallas kernels  16.5 us (49%)
  starting transfers between devices  15.8 us (47%)
  waiting for transfers between devices  0.61 us (2%)
    pallas_call x5, Pallas kernels, call(): pl.pallas_call(kernel, grid=(1,) if form == 'block' else (), in_specs=[fr...  14.1 us
    ppermute x1, starting transfers between devices, per_device(): right = lax.ppermute(to_left, axes, [(b, a) for a, b in steps])  6.03 us
    ppermute x3, starting transfers between devices, across(): return lax.ppermute(values, axes, pairs)  4.73 us
    all_to_all x1, starting transfers between devices, per_device(): lax.all_to_all(rows_out, 'tile', split_axis=0, concat_axis=0, tiled=True)  3.97 us
    pallas_call x1, Pallas kernels, per_device(): pl.pallas_call(out_kernel, grid=(1,), in_specs=[pl.BlockSpec((fields, 8,...  2.36 us
    ppermute x1, starting transfers between devices, per_device(): left = lax.ppermute(to_right, axes, steps)  1.11 us
  transfers between devices with their start and end apart: 6, of which 1 were waited for; matrix products, arithmetic and copies ran while one was open for 0% of the time, Pallas kernels for 36%

profile of v6, /device:TPU:1, one launch (start us, length us, event | category | flops | bytes accessed | tf_op | source)
XLA Modules:
  0.0 33.3 jit_solution(15640530386975376466)
XLA Ops:
  0.0 0.0 copy-start
  0.0 0.0 copy-start.5
  0.0 0.0 copy-start.6
  0.0 2.4 %shard_map.92 = f32[32,4,128]{2,1,0:T(4,128)} custom-call(f32[3,64,2048]{2,1,0:T(8,128)} %bitcast.11, s32[32,2,128]{2,1,0:T(2,128)} %bitcast.20, f32[32,128]{1,0:T(8,128)} %bitcast.21), custom_call_target="tpu_custom_call" | custom-call | tf_op jit(solution)/shard_map/pallas_call | solution.py:403
  2.4 4.3 %collective-permute-start = (f32[32,4,128]{2,1,0:T(4,128)}, f32[32,4,128]{2,1,0:T(4,128)S(1)}, u32[]{:S(2)}, u32[]{:S(2)}) collective-permute-start(f32[32,4,128]{2,1,0:T(4,128)} %shard_map.92), channel_id=1, source_target_pairs={{0,96},{1,97},{2,98},{3,99},{4,100},{5,101},{6,102},{7,103},{8,104... | collective-permute-start | bytes 196616 | tf_op jit(solution)/shard_map/ppermute | solution.py:417
  6.7 0.0 collective-permute-start.1
  6.7 0.4 %collective-permute-start.2 = (f32[32,4,128]{2,1,0:T(4,128)}, f32[32,4,128]{2,1,0:T(4,128)S(1)}, u32[]{:S(2)}, u32[]{:S(2)}) collective-permute-start(f32[32,4,128]{2,1,0:T(4,128)} %shard_map.92), channel_id=1, source_target_pairs={{0,32},{1,33},{2,34},{3,35},{4,36},{5,37},{6,38},{7,39},{8,40},{9,... | collective-permute-start | bytes 196616 | tf_op jit(solution)/shard_map/ppermute | solution.py:417
  7.1 0.0 copy-done
  7.1 0.0 copy-done.5
  7.1 0.0 copy-done.6
  7.1 0.0 copy-start.1
  7.1 0.0 copy-start.2
  7.1 0.0 copy-start.3
  7.1 0.0 copy-start.4
  7.2 2.6 %shard_map.91 = (f32[192,2048]{1,0:T(8,128)S(1)}, f32[192,128]{1,0:T(8,128)S(1)}, f32[192,128]{1,0:T(8,128)S(1)}) custom-call(f32[192,2048]{1,0:T(8,128)S(1)} %bitcast.12, f32[1,2048]{1,0:T(1,128)S(1)} %bitcast.17, s32[2,128]{1,0:T(2,128)S(1)} %bitcast.19), custom_call_target="tpu_custom_call" | custom-call | flops 4000000000 | bytes 4000000 | tf_op jit(solution)/shard_map/pallas_call | solution.py:367
  9.8 1.1 %collective-permute-start.3 = (f32[192,128]{1,0:T(8,128)S(1)}, f32[192,128]{1,0:T(8,128)S(1)}, u32[]{:S(2)}, u32[]{:S(2)}) collective-permute-start(f32[192,128]{1,0:T(8,128)S(1)} %get-tuple-element.15.after), channel_id=1, source_target_pairs={{0,1},{1,2},{2,3},{3,4},{4,5},{5,6},{6,7},{7,8},{8,9},{9,10},{10,1... | collective-permute-start | bytes 294920 | tf_op jit(solution)/shard_map/ppermute | solution.py:433
  10.9 6.0 %collective-permute-start.4 = (f32[192,128]{1,0:T(8,128)S(1)}, f32[192,128]{1,0:T(8,128)S(1)}, u32[]{:S(2)}, u32[]{:S(2)}) collective-permute-start(f32[192,128]{1,0:T(8,128)S(1)} %get-tuple-element.17), channel_id=1, source_target_pairs={{1,0},{2,1},{3,2},{4,3},{5,4},{6,5},{7,6},{8,7},{9,8},{10,9},{11,1... | collective-permute-start | bytes 294920 | tf_op jit(solution)/shard_map/ppermute | solution.py:434
  16.9 0.0 collective-permute-done.got0
  16.9 0.0 collective-permute-done.1.got1
  16.9 0.0 collective-permute-done.2.got2
  16.9 0.0 copy-done.1
  16.9 0.0 copy-done.2
  16.9 1.4 %shard_map.93.after = f32[32,12,128]{2,1,0:T(8,128)} custom-call(f32[32,4,128]{2,1,0:T(4,128)S(1)} %collective-permute-done.got0, f32[32,4,128]{2,1,0:T(4,128)S(1)} %collective-permute-done.1.got1, f32[32,4,128]{2,1,0:T(4,128)S(1)} %collective-permute-done.2.got2, s32[32,2,128]{2,1,0:T(2,128)S(1)} %bitcast.13, f32[32,128]{1,0:T(8,128)S(1)} %bitcast.14, ...), custom_call_target="tpu_custom_call" | custom-call | tf_op jit(solution)/shard_map/pallas_call | solution.py:367
  18.4 4.0 %all-to-all-start = ((f32[32,12,128]{2,1,0:T(8,128)}), f32[32,12,128]{2,1,0:T(8,128)S(1)}, u32[]{:S(2)}, u32[]{:S(2)}) async-start(f32[32,12,128]{2,1,0:T(8,128)} %shard_map.93.after), calls=%async_computation | async-start | bytes 524288 | tf_op jit(solution)/shard_map/all_to_all | solution.py:441
  22.4 0.0 copy-done.3
  22.4 0.0 copy-done.4
  22.4 6.1 %shard_map.94 = (f32[192,2048]{1,0:T(8,128)S(1)}, f32[1,2048]{1,0:T(1,128)S(1)}, s32[6,1,2048]{2,1,0:T(1,128)S(1)}, f32[64,64]{1,0:T(8,128)S(1)}) custom-call(f32[192,2048]{1,0:T(8,128)S(1)} %get-tuple-element.14.state, f32[1,2048]{1,0:T(1,128)S(1)} %bitcast.18, s32[6,1,2048]{2,1,0:T(1,128)S(1)} %bitcast.15, ...), custom_call_target="tpu_custom_call", output_to_operand_aliasing={{0}: (0, {})} | custom-call | flops 8000000000 | bytes 4000000 | tf_op jit(solution)/shard_map/pallas_call | solution.py:367
  28.5 0.0 collective-permute-done.3.left
  28.5 0.0 collective-permute-done.4.right
  28.5 2.0 %shard_map.95 = (f32[192,2048]{1,0:T(8,128)S(1)}, f32[64,64]{1,0:T(8,128)S(1)}) custom-call(f32[192,2048]{1,0:T(8,128)S(1)} %get-tuple-element.16.partial, f32[192,128]{1,0:T(8,128)S(1)} %collective-permute-done.3.left, f32[192,128]{1,0:T(8,128)S(1)} %collective-permute-done.4.right, ...), custom_call_target="tpu_custom_call", output_to_operand_aliasing={{0}: (0, {})} | custom-call | tf_op jit(solution)/shard_map/pallas_call | solution.py:367
  30.5 0.6 %all-to-all-done.got = f32[32,12,128]{2,1,0:T(8,128)S(1)} async-done(((f32[32,12,128]{2,1,0:T(8,128)}), f32[32,12,128]{2,1,0:T(8,128)S(1)}, u32[]{:S(2)}, u32[]{:S(2)}) %all-to-all-start) | async-done | bytes 196640 | tf_op jit(solution)/shard_map/all_to_all | solution.py:441
  31.1 2.0 %shard_map.96 = f32[192,2048]{1,0:T(8,128)} custom-call(f32[192,2048]{1,0:T(8,128)S(1)} %get-tuple-element.21.mixed, f32[32,12,128]{2,1,0:T(8,128)S(1)} %all-to-all-done.got, f32[64,64]{1,0:T(8,128)S(1)} %get-tuple-element.22.column), custom_call_target="tpu_custom_call" | custom-call | tf_op jit(solution)/shard_map/pallas_call | solution.py:367
Async XLA Ops:
  0.0 7.1 %copy-start = (f32[1,1,3,64,2048]{4,3,2,1,0:T(8,128)S(1)}, f32[1,1,3,64,2048]{4,3,2,1,0:T(8,128)}, u32[]{:S(2)}) copy-start(f32[1,1,3,64,2048]{4,3,2,1,0:T(8,128)} %param.9) | copy-start | bytes 4718596
  0.0 7.1 %copy-start.5 = (f32[1,1,2048]{2,1,0:T(1,128)S(1)}, f32[1,1,2048]{2,1,0:T(1,128)}, u32[]{:S(2)}) copy-start(f32[1,1,2048]{2,1,0:T(1,128)} %param.10) | copy-start | bytes 24580
  0.0 7.1 %copy-start.6 = (s32[1,1,2,128]{3,2,1,0:T(2,128)S(1)}, s32[1,1,2,128]{3,2,1,0:T(2,128)}, u32[]{:S(2)}) copy-start(s32[1,1,2,128]{3,2,1,0:T(2,128)} %param.13) | copy-start | bytes 3076
  2.4 14.6 %collective-permute-start = (f32[32,4,128]{2,1,0:T(4,128)}, f32[32,4,128]{2,1,0:T(4,128)S(1)}, u32[]{:S(2)}, u32[]{:S(2)}) collective-permute-start(f32[32,4,128]{2,1,0:T(4,128)} %shard_map.92), channel_id=1, source_target_pairs={{0,96},{1,97},{2,98},{3,99},{4,100},{5,101},{6,102},{7,103},{8,104... | collective-permute-start | bytes 196616 | tf_op jit(solution)/shard_map/ppermute | solution.py:417
  6.7 10.2 %collective-permute-start.1 = (f32[32,4,128]{2,1,0:T(4,128)}, f32[32,4,128]{2,1,0:T(4,128)S(1)}, u32[]{:S(2)}, u32[]{:S(2)}) collective-permute-start(f32[32,4,128]{2,1,0:T(4,128)} %shard_map.92), channel_id=1, source_target_pairs={{0,64},{1,65},{2,66},{3,67},{4,68},{5,69},{6,70},{7,71},{8,72},{9,... | collective-permute-start | bytes 196616 | tf_op jit(solution)/shard_map/ppermute | solution.py:417
  6.7 10.2 %collective-permute-start.2 = (f32[32,4,128]{2,1,0:T(4,128)}, f32[32,4,128]{2,1,0:T(4,128)S(1)}, u32[]{:S(2)}, u32[]{:S(2)}) collective-permute-start(f32[32,4,128]{2,1,0:T(4,128)} %shard_map.92), channel_id=1, source_target_pairs={{0,32},{1,33},{2,34},{3,35},{4,36},{5,37},{6,38},{7,39},{8,40},{9,... | collective-permute-start | bytes 196616 | tf_op jit(solution)/shard_map/ppermute | solution.py:417
  7.1 9.8 %copy-start.1 = (s32[1,1,32,2,128]{4,3,2,1,0:T(2,128)S(1)}, s32[1,1,32,2,128]{4,3,2,1,0:T(2,128)}, u32[]{:S(2)}) copy-start(s32[1,1,32,2,128]{4,3,2,1,0:T(2,128)} %param.16) | copy-start | bytes 98308
  7.1 9.8 %copy-start.2 = (f32[1,1,32,128]{3,2,1,0:T(8,128)S(1)}, f32[1,1,32,128]{3,2,1,0:T(8,128)}, u32[]{:S(2)}) copy-start(f32[1,1,32,128]{3,2,1,0:T(8,128)} %param.17) | copy-start | bytes 49156
  7.1 15.2 %copy-start.3 = (s32[1,1,6,2048]{3,1,2,0:T(1,128)S(1)}, s32[1,1,6,2048]{3,1,2,0:T(1,128)}, u32[]{:S(2)}) copy-start(s32[1,1,6,2048]{3,1,2,0:T(1,128)} %param.12) | copy-start | bytes 147460
  7.1 15.2 %copy-start.4 = (f32[1,64,64]{2,1,0:T(8,128)S(1)}, f32[1,64,64]{2,1,0:T(8,128)}, u32[]{:S(2)}) copy-start(f32[1,64,64]{2,1,0:T(8,128)} %param.11) | copy-start | bytes 49156
  9.8 18.7 %collective-permute-start.3 = (f32[192,128]{1,0:T(8,128)S(1)}, f32[192,128]{1,0:T(8,128)S(1)}, u32[]{:S(2)}, u32[]{:S(2)}) collective-permute-start(f32[192,128]{1,0:T(8,128)S(1)} %get-tuple-element.15.after), channel_id=1, source_target_pairs={{0,1},{1,2},{2,3},{3,4},{4,5},{5,6},{6,7},{7,8},{8,9},{9,10},{10,1... | collective-permute-start | bytes 294920 | tf_op jit(solution)/shard_map/ppermute | solution.py:433
  10.9 17.6 %collective-permute-start.4 = (f32[192,128]{1,0:T(8,128)S(1)}, f32[192,128]{1,0:T(8,128)S(1)}, u32[]{:S(2)}, u32[]{:S(2)}) collective-permute-start(f32[192,128]{1,0:T(8,128)S(1)} %get-tuple-element.17), channel_id=1, source_target_pairs={{1,0},{2,1},{3,2},{4,3},{5,4},{6,5},{7,6},{8,7},{9,8},{10,9},{11,1... | collective-permute-start | bytes 294920 | tf_op jit(solution)/shard_map/ppermute | solution.py:434
  18.4 12.7 %all-to-all-start = ((f32[32,12,128]{2,1,0:T(8,128)}), f32[32,12,128]{2,1,0:T(8,128)S(1)}, u32[]{:S(2)}, u32[]{:S(2)}) async-start(f32[32,12,128]{2,1,0:T(8,128)} %shard_map.93.after), calls=%async_computation | async-start | bytes 524288 | tf_op jit(solution)/shard_map/all_to_all | solution.py:441
